TPU v7x, 128 devices: a whole 4x4x4 slice. The times are simulated.
128 devices in a mesh: grp: 16 (over z_lo, x, core), vocab: 8 (over y, z_hi).
Axes of the slice: x: 4, y: 4, z: 4 (z_hi: 2, z_lo: 2; z = z_hi * 2 + z_lo), core: 2. Of those that a mesh axis runs over, the one named last changes fastest.
Arguments:
- embedded: bfloat16 [512, 4, 5120], P('grp'), may hold values from -6 to 6
- attn_gain: float32 [5120], replicated, may hold values from 0.1 to 1.9
- query_weight: bfloat16 [5120, 4096], P(None, 'vocab'), may hold values from -0.078125 to 0.078125
- key_weight: bfloat16 [5120, 1024], P(None, 'vocab'), may hold values from -0.3125 to 0.3125
- value_weight: bfloat16 [5120, 1024], P(None, 'vocab'), may hold values from -0.078125 to 0.078125
- out_weight: bfloat16 [4096, 5120], P('vocab'), may hold values from -0.75 to 0.75
- final_gain: float32 [5120], replicated, may hold values from 0.5 to 1.5
- head_weight: bfloat16 [5120, 81920], P(None, ('grp', 'vocab')), may hold values from -3 to 3
- prefix_keys: bfloat16 [16, 8, 2048, 128], P('grp', 'vocab'), may hold values from -150 to 150
- prefix_values: bfloat16 [16, 8, 2048, 128], P('grp', 'vocab'), may hold values from -6 to 6
- sample_prompt: int32 [512], P('grp'), may hold values from 0 to 15, as said below
Outputs:
- log_probs: float32 [512, 4, 81920], P(None, None, ('grp', 'vocab'))
Inputs may be any that keep to these rules, and one draw needn't show every extreme that they name: `sample_prompt`: each device's aligned block of 32 samples holds exactly 2 samples of every one of the 16 prompts, in a drawn order.
All inputs are finite; a program needn't handle non-finite values.
Results may differ from a plain program's by a relative error of at most 0.0029.
The roundings to bfloat16 on the way count: a program that leaves them out, or rounds other values in their place, can miss the bound.
Values may be sent and summed in bfloat16 or wider, within the bound.
No kernel may reach another device: no remote copies, remote signals or barrier semaphores. Data moves between devices by JAX's collectives and lax.ppermute only.
A program may use at most 128 MiB of HBM per device.

v0:
```python
import functools

import jax
import jax.numpy as jnp
from jax import lax
from jax.experimental import pallas as pl
from jax.experimental.pallas import tpu as pltpu
from jax.sharding import PartitionSpec as P

BOTH = ("grp", "vocab")
RING = 4
PIECES = ((0, 1792), (1792, 3584), (3584, 5120))
ORDERS = ("xyz", "yzx", "zxy")


def place_of(flat):
    grp, vocab = divmod(flat, 8)
    z_lo, rest = divmod(grp, 8)
    x, core = divmod(rest, 2)
    y, z_hi = divmod(vocab, 2)
    return {"x": x, "y": y, "z": z_hi * 2 + z_lo, "core": core}


def flat_of(at):
    grp = (at["z"] % 2) * 8 + at["x"] * 2 + at["core"]
    return grp * 8 + at["y"] * 2 + at["z"] // 2


def chip_turn(at, core):
    return (at - core) % RING


def meet_pairs(axis, bit):
    pairs = []
    for source in range(128):
        at = place_of(source)
        at[axis] = ((chip_turn(at[axis], at["core"]) ^ bit) + at["core"]) % RING
        pairs.append((source, flat_of(at)))
    return pairs


def swap_pairs(axis, distance, size):
    pairs = []
    for source in range(128):
        at = place_of(source)
        at[axis] = (at[axis] + distance) % size
        pairs.append((source, flat_of(at)))
    return pairs


FAR = {axis: meet_pairs(axis, 2) for axis in "xyz"}
NEAR = {axis: meet_pairs(axis, 1) for axis in "xyz"}
CORES = swap_pairs("core", 1, 2)
HALVES = swap_pairs("z", 2, RING)


def swap_cores(block):
    return lax.ppermute(block, BOTH, CORES)


def meet_gather(blocks):
    held = list(blocks)

    def meet(parts, turn):
        pairs = FAR if turn < 3 else NEAR
        return [
            lax.ppermute(part, BOTH, pairs[order[turn % 3]]) for part, order in zip(parts, ORDERS)
        ]

    for turn in range(4):
        held = [jnp.stack(both) for both in zip(held, meet(held, turn))]
    fifth = meet(held, 4)
    sixth = meet(held, 5)
    fifth = list(lax.optimization_barrier(tuple(fifth)))
    return list(zip(held, fifth)), list(zip(sixth, meet(fifth, 5)))


def weight_copies(k, own_w, other_w, weights, sems):
    a, b = PIECES[k]
    half = own_w.shape[1]
    rows = pl.ds(a, b - a)
    return [
        pltpu.make_async_copy(own_w.at[rows], weights[k].at[:, pl.ds(0, half)], sems.at[k, 0]),
        pltpu.make_async_copy(other_w.at[rows], weights[k].at[:, pl.ds(half, half)], sems.at[k, 1]),
    ]


def head_kernel(mark, *refs):
    parts, (own_w, other_w), refs = (refs[0:2], refs[2:4], refs[4:6]), refs[6:8], refs[8:]
    if mark == 0:
        (out,), work = refs[:1], refs[1:]
    else:
        (before, own_out, other_out, sums), work = refs[:4], refs[4:]
    lhs, weights, (total, lhs_sem, w_sem, in_sem, out_sem) = work[0:3], work[3:6], work[6:]
    mine, cols = total.shape[4:]
    half = own_w.shape[1]

    def copies(k):
        room, sem = lhs[k], lhs_sem.at[k]
        moves = []
        for h, part in enumerate(parts[k]):
            if k == 0:
                moves.append((part, room.at[h]))
            elif k == 1:
                moves += [(part.at[:, x], room.at[h, :, :, :, x]) for x in range(2)]
            else:
                moves += [(part.at[:, :, :, z], room.at[:, h, z]) for z in range(2)]
        return [
            pltpu.make_async_copy(source, to, sem.at[i]) for i, (source, to) in enumerate(moves)
        ] + weight_copies(k, own_w, other_w, weights, w_sem)

    def begin(k):
        for copy in copies(k):
            copy.start()

    def product(k):
        for copy in copies(k):
            copy.wait()
        if k < 2:
            begin(k + 1)
        rows = lhs[k][...].reshape(32 * mine, -1)
        fresh = jnp.dot(rows, weights[k][...], preferred_element_type=jnp.float32)
        return fresh.reshape(2, 2, 8, mine, cols)

    begin(0)
    if mark == 0:
        total[0] = product(0)
        total[1] = jnp.zeros(total.shape[1:], jnp.float32)
    else:
        load = pltpu.make_async_copy(before, total, in_sem)
        load.start()
        fresh = product(0)
        load.wait()
        total[1] += fresh
    def out_copies(z, y):
        if mark == 0:
            return [pltpu.make_async_copy(total.at[z, y], out.at[z, y], out_sem.at[z, y, 0])]
        return [
            pltpu.make_async_copy(
                total.at[z, y, :, :, :, pl.ds(at * half, half)], ref.at[z, y], out_sem.at[z, y, at]
            )
            for at, ref in enumerate((own_out, other_out))
        ]

    def finish(z, y):
        for copy in out_copies(z, y):
            copy.start()
        if mark == 1:
            rows = total[z, y].reshape(16 * mine, cols)
            top = jnp.max(rows, axis=1, keepdims=True)
            mass = jnp.sum(jnp.exp(rows - top), axis=1, keepdims=True)
            at = pl.ds(pl.multiple_of((z * 2 + y) * 16 * mine, 16 * mine), 16 * mine)
            sums[at] = top + jnp.log(mass)

    total[:, :, mark] += product(1)
    for z in range(2):
        finish(z, 1 - mark)
    total[:, mark] += product(2)
    for z in range(2):
        finish(z, mark)
    for z in range(2):
        for y in range(2):
            for copy in out_copies(z, y):
                copy.wait()


def head_logits(held, taken, own_w, other_w, mine):
    half = own_w.shape[1]
    rows = 64 * mine
    anywhere = pl.BlockSpec(memory_space=pl.ANY)
    widths = [b - a for a, b in PIECES]
    shape = (2, 2, 2, 8, mine)
    flops = rows * 5120 * 2 * half

    def call(mark, out_shape, out_specs, operands):
        return pl.pallas_call(
            functools.partial(head_kernel, mark),
            out_shape=out_shape,
            in_specs=[anywhere] * len(operands),
            out_specs=out_specs,
            scratch_shapes=[pltpu.VMEM((2, 2, 2, 2, 2, mine, w), jnp.bfloat16) for w in widths]
            + [pltpu.VMEM((w, 2 * half), jnp.bfloat16) for w in widths]
            + [
                pltpu.VMEM(shape + (2 * half,), jnp.float32),
                pltpu.SemaphoreType.DMA((3, 4)),
                pltpu.SemaphoreType.DMA((3, 2)),
                pltpu.SemaphoreType.DMA,
                pltpu.SemaphoreType.DMA((2, 2, 2)),
            ],
            compiler_params=pltpu.CompilerParams(vmem_limit_bytes=48 * 2**20),
            cost_estimate=pl.CostEstimate(
                flops=flops, bytes_accessed=26 * 10**6, transcendentals=mark * rows * 2 * half
            ),
            name=("head_early", "head_late")[mark],
        )(*operands)

    early = call(
        0,
        jax.ShapeDtypeStruct(shape + (2 * half,), jnp.float32),
        anywhere,
        [half for piece in held for half in piece] + [own_w, other_w],
    )
    return call(
        1,
        (
            jax.ShapeDtypeStruct(shape + (half,), jnp.float32),
            jax.ShapeDtypeStruct(shape + (half,), jnp.float32),
            jax.ShapeDtypeStruct((rows, 1), jnp.float32),
        ),
        (anywhere, anywhere, pl.BlockSpec(memory_space=pltpu.VMEM)),
        [half for piece in taken for half in piece] + [own_w, other_w, early],
    )


def front_kernel(
    prompts, column, embedded, gain, query_w, key_w, value_w, out, order, seen, raw, weights, sems
):
    samples, steps, width = embedded.shape
    cuts = (0, query_w.shape[1], query_w.shape[1] + key_w.shape[1])
    copies = [
        pltpu.make_async_copy(w, weights.at[:, pl.ds(at, w.shape[1])], sems.at[i])
        for i, (w, at) in enumerate(zip((query_w, key_w, value_w), cuts))
    ]
    for copy in copies:
        copy.start()
    for p in range(samples // 2):
        seen[p] = 0
    for i in range(samples):
        p = prompts[i]
        slot = p * 2 + seen[p]
        seen[p] = seen[p] + 1
        order[slot] = i
    for slot in range(samples):
        raw[slot * steps : (slot + 1) * steps] = embedded[order[slot]].astype(jnp.float32)
    rows = raw[...]
    mean_sq = jnp.mean(rows * rows, axis=-1, keepdims=True)
    normed = (rows * lax.rsqrt(mean_sq + 1e-06) * gain[...]).astype(jnp.bfloat16)
    span = out.shape[1] - weights.shape[1]
    at = pl.multiple_of(column[0], 128)
    out[:, weights.shape[1] :] = raw[:, pl.ds(at, span)].astype(jnp.bfloat16)
    for copy in copies:
        copy.wait()
    out[:, : weights.shape[1]] = jnp.dot(
        normed, weights[...], preferred_element_type=jnp.float32
    ).astype(jnp.bfloat16)


def front(sample_prompt, column, embedded, gain, query_w, key_w, value_w, span):
    samples, steps, width = embedded.shape
    anywhere = pl.BlockSpec(memory_space=pl.ANY)
    scalars = pl.BlockSpec(memory_space=pltpu.SMEM)
    vector = pl.BlockSpec(memory_space=pltpu.VMEM)
    cols = query_w.shape[1] + key_w.shape[1] + value_w.shape[1]
    return pl.pallas_call(
        front_kernel,
        out_shape=(
            jax.ShapeDtypeStruct((samples * steps, cols + span), jnp.bfloat16),
            jax.ShapeDtypeStruct((samples,), jnp.int32),
        ),
        in_specs=[scalars, scalars, vector, vector, anywhere, anywhere, anywhere],
        out_specs=(vector, scalars),
        scratch_shapes=[
            pltpu.SMEM((samples // 2,), jnp.int32),
            pltpu.VMEM((samples * steps, width), jnp.float32),
            pltpu.VMEM((width, cols), jnp.bfloat16),
            pltpu.SemaphoreType.DMA((3,)),
        ],
        compiler_params=pltpu.CompilerParams(vmem_limit_bytes=60 * 2**20),
        cost_estimate=pl.CostEstimate(
            flops=2 * samples * steps * width * cols, bytes_accessed=10**7, transcendentals=0
        ),
        name="front",
    )(sample_prompt, column, embedded, gain.reshape(1, -1), query_w, key_w, value_w)


def attend_kernel(steps, local, keys, values, out):
    head = keys.shape[1]
    rows = local.shape[0]
    groups = out.shape[1] // head
    scale = 1.0 / head**0.5
    new_keys = local[:, groups * head : (groups + 1) * head]
    new_values = local[:, (groups + 1) * head : (groups + 2) * head]
    at_row = lax.broadcasted_iota(jnp.int32, (rows, rows), 0)
    at_col = lax.broadcasted_iota(jnp.int32, (rows, rows), 1)
    seen = (at_row // steps == at_col // steps) & (at_col <= at_row)
    across = (((1,), (1,)), ((), ()))

    def parts(scores, value_rows):
        peak = jnp.max(scores, axis=1, keepdims=True)
        powers = jnp.exp(scores - peak)
        weighted = jnp.dot(
            powers.astype(jnp.bfloat16), value_rows, preferred_element_type=jnp.float32
        )
        return peak, jnp.sum(powers, axis=1, keepdims=True), weighted

    for g in range(groups):
        span = slice(g * head, (g + 1) * head)
        queries = local[:, span]
        scores = lax.dot_general(queries, keys[...], across, preferred_element_type=jnp.float32)
        prefix_peak, prefix_total, prefix_sum = parts(scores * scale, values[...])
        scores = lax.dot_general(queries, new_keys, across, preferred_element_type=jnp.float32)
        new_peak, new_total, new_sum = parts(jnp.where(seen, scores * scale, -1e30), new_values)
        peak = jnp.maximum(prefix_peak, new_peak)
        prefix_factor = jnp.exp(prefix_peak - peak)
        new_factor = jnp.exp(new_peak - peak)
        total = prefix_total * prefix_factor + new_total * new_factor
        attended = (prefix_sum * prefix_factor + new_sum * new_factor) / total
        out[:, span] = attended.astype(jnp.bfloat16)


def attend(local, keys, values, steps, cols):
    vector = pl.BlockSpec(memory_space=pltpu.VMEM)
    return pl.pallas_call(
        functools.partial(attend_kernel, steps),
        out_shape=jax.ShapeDtypeStruct((local.shape[0], cols), jnp.bfloat16),
        in_specs=[vector] * 3,
        out_specs=vector,
        compiler_params=pltpu.CompilerParams(vmem_limit_bytes=40 * 2**20),
        name="attend",
    )(local, keys, values)


def output_kernel(order, place, own, other, totals, out):
    pair = pl.program_id(0)
    y, z_hi = pair // 2, pair % 2
    core, x_here, y_here, z_here = place[0], place[1], place[2], place[3]
    for ref, plane in ((own, core), (other, 1 - core)):
        turn = lambda at: (at - plane) & 3
        apart = lambda here, there: turn(here) ^ turn(there)
        for z_lo in range(2):
            for x in range(4):
                prompt = z_lo * 8 + x * 2 + plane
                dz, dy, dx = apart(z_here, z_hi * 2 + z_lo), apart(y_here, y), apart(x_here, x)
                far = (dz >> 1) * 4 + (dy >> 1) * 2 + (dx >> 1)
                block = ref[dz & 1, dy & 1, dx & 1, far] - totals[prompt, pair]
                for row in range(4):
                    near, which = divmod(row, 2)
                    to = order[(pair * 2 + near) * 32 + prompt * 2 + which]
                    out[near * 32 + to] = block[row * 4 : row * 4 + 4]


def ordered_output(order, place, own, other, totals):
    width = own.shape[-1]
    whole = lambda a: pl.BlockSpec(a.shape, lambda i, *_: (0,) * a.ndim)
    return pl.pallas_call(
        output_kernel,
        out_shape=jax.ShapeDtypeStruct((512, 4, width), jnp.float32),
        grid_spec=pltpu.PrefetchScalarGridSpec(
            num_scalar_prefetch=2,
            grid=(8,),
            in_specs=[whole(own), whole(other), whole(totals)],
            out_specs=pl.BlockSpec((64, 4, width), lambda i, *_: (i, 0, 0)),
        ),
        compiler_params=pltpu.CompilerParams(vmem_limit_bytes=52 * 2**20),
        name="output",
    )(order, place, own, other, totals)


def rms_scale(rows, gain):
    mean_sq = jnp.mean(rows * rows, axis=-1, keepdims=True)
    return rows * lax.rsqrt(mean_sq + 1e-06) * gain


def log_sum(values, axis):
    top = jnp.max(values, axis=axis, keepdims=True)
    return jnp.squeeze(top, axis) + jnp.log(jnp.sum(jnp.exp(values - top), axis=axis))


def spread(values, axis):
    copies = lax.axis_size(axis)
    return lax.all_to_all(
        jnp.broadcast_to(values[None], (copies,) + values.shape), axis, 0, 0, tiled=True
    )


def on_device(
    embedded,
    attn_gain,
    query_weight,
    key_weight,
    value_weight,
    out_weight,
    final_gain,
    head_weight,
    prefix_keys,
    prefix_values,
    sample_prompt,
):
    samples, steps, width = embedded.shape
    rows = samples * steps
    cols = query_weight.shape[1]
    core = lax.axis_index("grp") % 2
    z_hi = lax.axis_index("vocab") % 2
    z = z_hi * 2 + lax.axis_index("grp") // 8
    y = lax.axis_index("vocab") // 2
    x = (lax.axis_index("grp") // 2) % 4
    shares = lax.axis_size("vocab")
    mine = rows // shares
    span = width // shares
    half = width // 2
    other_weight = swap_cores(head_weight)

    own_columns = lax.axis_index("vocab") * span
    sorted_rows, sample_at = front(
        sample_prompt,
        own_columns.reshape(1).astype(jnp.int32),
        embedded,
        attn_gain,
        query_weight,
        key_weight,
        value_weight,
        span,
    )
    local = lax.all_to_all(sorted_rows, "grp", 0, 0, tiled=True)

    attended = attend(local, prefix_keys[0, 0], prefix_values[0, 0], steps, cols)
    attended, other_weight = lax.optimization_barrier((attended, other_weight))
    own_embedded = local[:, -span:].astype(jnp.float32)

    def product(part, attended):
        w = lax.slice_in_dim(out_weight, part * half, (part + 1) * half, axis=1)
        full = jnp.dot(attended, w, preferred_element_type=jnp.float32)
        at = (y * 2 + z_hi) % 4 * span
        chunk = lax.dynamic_slice_in_dim(full, at, span, 1)
        chunk = jnp.where((y * 2 + z_hi) // 4 == part, chunk + own_embedded, chunk)
        return lax.dynamic_update_slice_in_dim(full, chunk, at, 1)

    both = jnp.concatenate([product(0, attended), product(1, attended)], axis=1)
    arrived = lax.all_to_all(both, "vocab", 0, 0, tiled=True)
    hidden = jnp.sum(arrived.reshape(shares, mine, width), axis=0)
    normed = rms_scale(hidden, final_gain).astype(jnp.bfloat16)

    held, taken = meet_gather([normed[:, a:b] for a, b in PIECES])
    logits, other_logits, local_sum = head_logits(held, taken, head_weight, other_weight, mine)
    crossed = swap_cores(other_logits)

    places = jnp.arange(RING, dtype=jnp.int32)
    apart = lambda at: chip_turn(at, core) ^ chip_turn(places, core)
    dz, dy, dx = apart(z)[:, None, None], apart(y)[None, :, None], apart(x)[None, None, :]
    nears = (dz & 1) * 4 + (dy & 1) * 2 + (dx & 1)
    fars = (dz >> 1) * 4 + (dy >> 1) * 2 + (dx >> 1)
    mine_order = (nears * 8 + fars).reshape(64)
    local_sum = jnp.take(local_sum.reshape(64, mine), mine_order, axis=0)
    over_vocab = log_sum(spread(local_sum.reshape(64 * mine), "vocab"), 0)
    sent = jnp.concatenate([over_vocab, sample_at.astype(jnp.float32)])
    over_grp = spread(sent, "grp")
    order = over_grp[:, 64 * mine :].astype(jnp.int32).reshape(-1)
    total = log_sum(over_grp[:, : 64 * mine].reshape(8, 2, 64 * mine), 0)
    total = total.reshape(2, 2, 2, 4, 4, mine).transpose(2, 4, 0, 3, 1, 5)
    return ordered_output(
        order,
        jnp.stack([core, x, y, z]).astype(jnp.int32),
        logits,
        crossed,
        total.reshape(16, 8, mine, 1),
    )


def solution(mesh):
    placed = (
        P("grp", None, None),
        P(),
        P(None, "vocab"),
        P(None, "vocab"),
        P(None, "vocab"),
        P("vocab", None),
        P(),
        P(None, ("grp", "vocab")),
        P("grp", "vocab", None, None),
        P("grp", "vocab", None, None),
        P("grp"),
    )
    return jax.shard_map(
        on_device,
        mesh=mesh,
        in_specs=placed,
        out_specs=P(None, None, ("grp", "vocab")),
        check_vma=False,
    )
```

profile of v0, /device:TPU:1, one launch (start us, length us, event | category | flops | bytes accessed | tf_op | source)
XLA Modules:
  0.0 190.3 jit_solution(13314832973806376208)
XLA Ops:
  0.0 1.4 collective-permute-start
  1.4 7.1 %front.1 = (bf16[128,1408]{1,0:T(8,128)(2,1)}, s32[32]{0:T(128)}) custom-call(s32[32]{0:T(128)} %prompts.1, s32[1]{0:T(128)} %bitcast.column, bf16[32,4,5120]{2,1,0:T(4,128)(2,1)} %embedded.1, f32[1,5120]{1,0:T(1,128)} %bitcast.84, bf16[5120,512]{1,0:T(8,128)(2,1)} %query_w.1, bf16[5120,128]{1,0:T(8,128)(2,1)} %key_w.1, bf16[5120,128]{1,0:T(8,128)(2,1)} %value_w.1), custom_call_target="tpu_custom_call" | custom-call | flops 1006632960 | bytes 10000000 | tf_op jit(solution)/shard_map/front/pallas_call | solution.py:254
  8.6 5.9 %all-to-all-start = ((bf16[16,8,1408]{2,1,0:T(8,128)(2,1)}), bf16[16,8,1408]{2,1,0:T(8,128)(2,1)S(1)}, u32[]{:S(2)}, u32[]{:S(2)}) async-start(bf16[16,8,1408]{2,1,0:T(8,128)(2,1)} %bitcast.70), calls=%async_computation | async-start | bytes 720896 | tf_op jit(solution)/shard_map/all_to_all | solution.py:414
  14.4 7.9 %all-to-all-done = bf16[16,8,1408]{2,1,0:T(8,128)(2,1)S(1)} async-done(((bf16[16,8,1408]{2,1,0:T(8,128)(2,1)}), bf16[16,8,1408]{2,1,0:T(8,128)(2,1)S(1)}, u32[]{:S(2)}, u32[]{:S(2)}) %all-to-all-start) | async-done | bytes 360480 | tf_op jit(solution)/shard_map/all_to_all | solution.py:414
  22.4 3.2 %attend.1 = bf16[128,512]{1,0:T(8,128)(2,1)S(1)} custom-call(bf16[128,1408]{1,0:T(8,128)(2,1)S(1)} %bitcast.62, bf16[2048,128]{1,0:T(8,128)(2,1)S(1)} %bitcast.64, bf16[2048,128]{1,0:T(8,128)(2,1)S(1)} %bitcast.65), custom_call_target="tpu_custom_call" | custom-call | tf_op jit(solution)/shard_map/attend/pallas_call | solution.py:313
  25.6 2.2 %fusion.2 = f32[128,2560]{1,0:T(8,128)S(1)} fusion(bf16[128,512]{1,0:T(8,128)(2,1)S(1)} %attend.1, bf16[512,5120]{1,0:T(8,128)(2,1)} %param.16), kind=kOutput, calls=%fused_computation.4 | convolution fusion | flops 335544320 | bytes 4063232 | tf_op jit(solution)/shard_map/dot_general | solution.py:422
  28.7 38.8 %all_to_all.38 = f32[8,16,5120]{2,1,0:T(8,128)S(1)} all-to-all(f32[8,16,5120]{2,1,0:T(8,128)S(1)} %bitcast.66), channel_id=1, replica_groups=mesh['grp'=16,'vocab'=8] {'vocab'}, dimensions={0} | all-to-all | bytes 5242880 | tf_op jit(solution)/shard_map/all_to_all | solution.py:429
  68.4 1.6 collective-permute-start.12
  70.0 2.7 %collective-permute-start.1 = (bf16[16,1792]{1,0:T(8,128)(2,1)S(1)}, bf16[16,1792]{1,0:T(8,128)(2,1)S(1)}, u32[]{:S(2)}, u32[]{:S(2)}) collective-permute-start(bf16[16,1792]{1,0:T(8,128)(2,1)S(1)} %get-tuple-element.44), channel_id=1, source_target_pairs={{0,32},{1,33},{2,34},{3,35},{4,36},{5,37},{6,38},{7,39},{8,40},{9,... | collective-permute-start | bytes 172040 | tf_op jit(solution)/shard_map/ppermute | solution.py:67
  73.3 2.7 %collective-permute-start.13 = (bf16[2,16,1536]{2,1,0:T(8,128)(2,1)S(1)}, bf16[2,16,1536]{2,1,0:T(8,128)(2,1)S(1)}, u32[]{:S(2)}, u32[]{:S(2)}) collective-permute-start(bf16[2,16,1536]{2,1,0:T(8,128)(2,1)S(1)} %get-tuple-element.50), channel_id=1, source_target_pairs={{0,32},{1,33},{2,34},{3,35},{4,36},{5,37},{6,38},{7,39},{8,40},{9,... | collective-permute-start | bytes 294920 | tf_op jit(solution)/shard_map/ppermute | solution.py:67
  77.6 1.9 %collective-permute-start.8 = (bf16[2,16,1792]{2,1,0:T(8,128)(2,1)S(1)}, bf16[2,16,1792]{2,1,0:T(8,128)(2,1)S(1)}, u32[]{:S(2)}, u32[]{:S(2)}) collective-permute-start(bf16[2,16,1792]{2,1,0:T(8,128)(2,1)S(1)} %get-tuple-element.46), channel_id=1, source_target_pairs={{0,1},{1,0},{2,3},{3,2},{4,5},{5,4},{6,7},{7,6},{8,9},{9,8},{10,11... | collective-permute-start | bytes 344072 | tf_op jit(solution)/shard_map/ppermute | solution.py:67
  79.5 1.4 collective-permute-start.14
  81.3 1.5 collective-permute-start.3
  82.9 1.7 collective-permute-start.9
  84.6 4.0 %collective-permute-done.3 = bf16[2,2,16,1792]{3,2,1,0:T(8,128)(2,1)S(1)} collective-permute-done((bf16[2,2,16,1792]{3,2,1,0:T(8,128)(2,1)S(1)}, bf16[2,2,16,1792]{3,2,1,0:T(8,128)(2,1)S(1)}, u32[]{:S(2)}, u32[]{:S(2)}) %collective-permute-start.3) | collective-permute-done | bytes 229408 | tf_op jit(solution)/shard_map/ppermute | solution.py:67
  88.6 1.4 collective-permute-start.4
  90.1 1.5 collective-permute-start.10
  92.6 7.1 %collective-permute-done.4 = bf16[2,2,2,16,1792]{4,3,2,1,0:T(8,128)(2,1)S(1)} collective-permute-done((bf16[2,2,2,16,1792]{4,3,2,1,0:T(8,128)(2,1)S(1)}, bf16[2,2,2,16,1792]{4,3,2,1,0:T(8,128)(2,1)S(1)}, u32[]{:S(2)}, u32[]{:S(2)}) %collective-permute-start.4) | collective-permute-done | bytes 458784 | tf_op jit(solution)/shard_map/ppermute | solution.py:67
  101.1 1.3 collective-permute-start.11
  103.7 2.5 %collective-permute-start.20 = (bf16[2,2,2,2,16,1536]{5,4,3,2,1,0:T(8,128)(2,1)S(1)}, bf16[2,2,2,2,16,1536]{5,4,3,2,1,0:T(8,128)(2,1)}, u32[]{:S(2)}, u32[]{:S(2)}) collective-permute-start(bf16[2,2,2,2,16,1536]{5,4,3,2,1,0:T(8,128)(2,1)S(1)} %pad_maximum_fusion.3.refs_4_), channel_id=1, source_target_pairs={{0,2},{1,3},{2,0},{3,1},{4,6},{5,7},{6,4},{7,5},{8,14},{9,15},{10,... | collective-permute-start | bytes 2359304 | tf_op jit(solution)/shard_map/ppermute | solution.py:67
  107.1 7.7 %collective-permute-done.16.refs_5_ = bf16[2,2,2,2,16,1536]{5,4,3,2,1,0:T(8,128)(2,1)S(1)} collective-permute-done((bf16[2,2,2,2,16,1536]{5,4,3,2,1,0:T(8,128)(2,1)S(1)}, bf16[2,2,2,2,16,1536]{5,4,3,2,1,0:T(8,128)(2,1)S(1)}, u32[]{:S(2)}, u32[]{:S(2)}) %collective-permute-start.16) | collective-permute-done | bytes 786464 | tf_op jit(solution)/shard_map/ppermute | solution.py:67
  115.8 1.7 collective-permute-start.17
  117.5 1.6 collective-permute-start.19
  119.0 2.9 %collective-permute-done.20.refs_4_ = bf16[2,2,2,2,16,1536]{5,4,3,2,1,0:T(8,128)(2,1)} collective-permute-done((bf16[2,2,2,2,16,1536]{5,4,3,2,1,0:T(8,128)(2,1)S(1)}, bf16[2,2,2,2,16,1536]{5,4,3,2,1,0:T(8,128)(2,1)}, u32[]{:S(2)}, u32[]{:S(2)}) %collective-permute-start.20) | collective-permute-done | bytes 786464 | tf_op jit(solution)/shard_map/ppermute | solution.py:67
  124.2 14.5 %head_early.1.refs_8_ = f32[2,2,2,8,16,1280]{5,4,3,2,1,0:T(8,128)} custom-call(bf16[2,2,2,2,16,1792]{5,4,3,2,1,0:T(8,128)(2,1)S(1)} %pad_maximum_fusion.1.refs_0_, bf16[2,2,2,2,16,1792]{5,4,3,2,1,0:T(8,128)(2,1)S(1)} %collective-permute-done.6.refs_1_, bf16[2,2,2,2,16,1792]{5,4,3,2,1,0:T(8,128)(2,1)S(1)} %pad_maximum_fusion.2.refs_2_, ...), custom_call_target="tpu_custom_call" | custom-call | flops 6710886400 | bytes 26000000 | tf_op jit(solution)/shard_map/head_early/pallas_call | solution.py:176
  138.7 15.0 %head_late.1 = (f32[2,2,2,8,16,640]{5,4,3,2,1,0:T(8,128)}, f32[2,2,2,8,16,640]{5,4,3,2,1,0:T(8,128)}, f32[1024,1]{1,0:T(8,128)S(1)}) custom-call(bf16[2,2,2,2,16,1792]{5,4,3,2,1,0:T(8,128)(2,1)} %collective-permute-done.5.refs_0_, bf16[2,2,2,2,16,1792]{5,4,3,2,1,0:T(8,128)(2,1)} %collective-permute-done.17.refs_1_, ...), custom_call_target="tpu_custom_call" | custom-call | flops 6710886400 | bytes 26000000 | tf_op jit(solution)/shard_map/head_late/pallas_call | solution.py:176
  153.8 3.0 %collective-permute-start.22 = (f32[2,2,2,8,16,640]{5,4,3,2,1,0:T(8,128)}, f32[2,2,2,8,16,640]{5,4,3,2,1,0:T(8,128)}, u32[]{:S(2)}, u32[]{:S(2)}) collective-permute-start(f32[2,2,2,8,16,640]{5,4,3,2,1,0:T(8,128)} %get-tuple-element.24), channel_id=1, source_target_pairs={{0,8},{1,9},{2,10},{3,11},{4,12},{5,13},{6,14},{7,15},{8,0},{9,1},... | collective-permute-start | bytes 7864328 | tf_op jit(solution)/shard_map/ppermute | solution.py:58
  158.9 4.5 %all-to-all-start.2 = ((f32[8,1,1024]{2,1,0:T(1,128)}), f32[8,1,1024]{2,1,0:T(1,128)S(1)}, u32[]{:S(2)}, u32[]{:S(2)}) async-start(f32[8,1,1024]{2,1,0:T(1,128)} %broadcast_in_dim.16), calls=%async_computation.2 | async-start | bytes 65536 | tf_op jit(solution)/shard_map/all_to_all | solution.py:371
  163.4 6.6 %all-to-all-done.2 = f32[8,1,1024]{2,1,0:T(1,128)S(1)} async-done(((f32[8,1,1024]{2,1,0:T(1,128)}), f32[8,1,1024]{2,1,0:T(1,128)S(1)}, u32[]{:S(2)}, u32[]{:S(2)}) %all-to-all-start.2) | async-done | bytes 32800 | tf_op jit(solution)/shard_map/all_to_all | solution.py:371
  170.7 4.7 %all-to-all-start.3 = ((f32[16,1,1056]{2,1,0:T(1,128)}), f32[16,1,1056]{2,1,0:T(1,128)S(1)}, u32[]{:S(2)}, u32[]{:S(2)}) async-start(f32[16,1,1056]{2,1,0:T(1,128)} %broadcast_in_dim.17), calls=%async_computation.3 | async-start | bytes 147456 | tf_op jit(solution)/shard_map/all_to_all | solution.py:371
  175.6 5.8 %all-to-all-done.3 = f32[16,1,1056]{2,1,0:T(1,128)S(1)} async-done(((f32[16,1,1056]{2,1,0:T(1,128)}), f32[16,1,1056]{2,1,0:T(1,128)S(1)}, u32[]{:S(2)}, u32[]{:S(2)}) %all-to-all-start.3) | async-done | bytes 67616 | tf_op jit(solution)/shard_map/all_to_all | solution.py:371
  182.6 7.7 %output.1 = f32[512,4,640]{2,1,0:T(4,128)} custom-call(s32[512]{0:T(512)S(1)} %reshape.282.order, s32[4]{0:T(128)S(1)} %pad_add_fusion.place, f32[2,2,2,8,16,640]{5,4,3,2,1,0:T(8,128)} %get-tuple-element.23.own, f32[2,2,2,8,16,640]{5,4,3,2,1,0:T(8,128)} %collective-permute-done.22.other, f32[16,8,16,1]{3,2,1,0:T(8,128)S(1)} %copy.24.totals), custom_call_target="tpu_custom_call" | custom-call | tf_op jit(solution)/shard_map/output/pallas_call | solution.py:345
  (97 shorter events, 16.4 us)
Async XLA Ops:
  0.0 25.6 %collective-permute-start = (bf16[5120,640]{1,0:T(8,128)(2,1)}, bf16[5120,640]{1,0:T(8,128)(2,1)}, u32[]{:S(2)}, u32[]{:S(2)}) collective-permute-start(bf16[5120,640]{1,0:T(8,128)(2,1)} %refs_6_.3), channel_id=1, source_target_pairs={{0,8},{1,9},{2,10},{3,11},{4,12},{5,13},{6,14},{7,15},{8,0},{9,1},... | collective-permute-start | bytes 19660808 | tf_op jit(solution)/shard_map/ppermute | solution.py:58
  1.4 21.0 %copy-start = (bf16[1,1,2048,128]{3,2,1,0:T(8,128)(2,1)S(1)}, bf16[1,1,2048,128]{3,2,1,0:T(8,128)(2,1)}, u32[]{:S(2)}) copy-start(bf16[1,1,2048,128]{3,2,1,0:T(8,128)(2,1)} %param.19) | copy-start | bytes 1572868
  1.4 21.0 %copy-start.1 = (bf16[1,1,2048,128]{3,2,1,0:T(8,128)(2,1)S(1)}, bf16[1,1,2048,128]{3,2,1,0:T(8,128)(2,1)}, u32[]{:S(2)}) copy-start(bf16[1,1,2048,128]{3,2,1,0:T(8,128)(2,1)} %param.20) | copy-start | bytes 1572868
  8.6 13.8 %all-to-all-start = ((bf16[16,8,1408]{2,1,0:T(8,128)(2,1)}), bf16[16,8,1408]{2,1,0:T(8,128)(2,1)S(1)}, u32[]{:S(2)}, u32[]{:S(2)}) async-start(bf16[16,8,1408]{2,1,0:T(8,128)(2,1)} %bitcast.70), calls=%async_computation | async-start | bytes 720896 | tf_op jit(solution)/shard_map/all_to_all | solution.py:414
  22.4 5.5 %copy-start.4 = (bf16[512,5120]{1,0:T(8,128)(2,1)S(1)}, bf16[512,5120]{1,0:T(8,128)(2,1)}, u32[]{:S(2)}) copy-start(bf16[512,5120]{1,0:T(8,128)(2,1)} %param.16) | copy-start | bytes 15728644
  68.4 4.9 %collective-permute-start.12 = (bf16[16,1536]{1,0:T(8,128)(2,1)S(1)}, bf16[16,1536]{1,0:T(8,128)(2,1)S(1)}, u32[]{:S(2)}, u32[]{:S(2)}) collective-permute-start(bf16[16,1536]{1,0:T(8,128)(2,1)S(1)} %get-tuple-element.40), channel_id=1, source_target_pairs={{0,1},{1,0},{2,3},{3,2},{4,5},{5,4},{6,7},{7,6},{8,9},{9,8},{10,11... | collective-permute-start | bytes 147464 | tf_op jit(solution)/shard_map/ppermute | solution.py:67
  70.0 6.0 %collective-permute-start.1 = (bf16[16,1792]{1,0:T(8,128)(2,1)S(1)}, bf16[16,1792]{1,0:T(8,128)(2,1)S(1)}, u32[]{:S(2)}, u32[]{:S(2)}) collective-permute-start(bf16[16,1792]{1,0:T(8,128)(2,1)S(1)} %get-tuple-element.44), channel_id=1, source_target_pairs={{0,32},{1,33},{2,34},{3,35},{4,36},{5,37},{6,38},{7,39},{8,40},{9,... | collective-permute-start | bytes 172040 | tf_op jit(solution)/shard_map/ppermute | solution.py:67
  72.7 4.8 %collective-permute-start.7 = (bf16[16,1792]{1,0:T(8,128)(2,1)S(1)}, bf16[16,1792]{1,0:T(8,128)(2,1)S(1)}, u32[]{:S(2)}, u32[]{:S(2)}) collective-permute-start(bf16[16,1792]{1,0:T(8,128)(2,1)S(1)} %get-tuple-element.43), channel_id=1, source_target_pairs={{0,4},{1,5},{2,6},{3,7},{4,0},{5,1},{6,2},{7,3},{8,12},{9,13},{10,... | collective-permute-start | bytes 172040 | tf_op jit(solution)/shard_map/ppermute | solution.py:67
  73.3 6.2 %collective-permute-start.13 = (bf16[2,16,1536]{2,1,0:T(8,128)(2,1)S(1)}, bf16[2,16,1536]{2,1,0:T(8,128)(2,1)S(1)}, u32[]{:S(2)}, u32[]{:S(2)}) collective-permute-start(bf16[2,16,1536]{2,1,0:T(8,128)(2,1)S(1)} %get-tuple-element.50), channel_id=1, source_target_pairs={{0,32},{1,33},{2,34},{3,35},{4,36},{5,37},{6,38},{7,39},{8,40},{9,... | collective-permute-start | bytes 294920 | tf_op jit(solution)/shard_map/ppermute | solution.py:67
  76.1 5.2 %collective-permute-start.2 = (bf16[2,16,1792]{2,1,0:T(8,128)(2,1)S(1)}, bf16[2,16,1792]{2,1,0:T(8,128)(2,1)S(1)}, u32[]{:S(2)}, u32[]{:S(2)}) collective-permute-start(bf16[2,16,1792]{2,1,0:T(8,128)(2,1)S(1)} %get-tuple-element.48), channel_id=1, source_target_pairs={{0,4},{1,5},{2,6},{3,7},{4,0},{5,1},{6,2},{7,3},{8,12},{9,13},{10,... | collective-permute-start | bytes 344072 | tf_op jit(solution)/shard_map/ppermute | solution.py:67
  77.6 5.3 %collective-permute-start.8 = (bf16[2,16,1792]{2,1,0:T(8,128)(2,1)S(1)}, bf16[2,16,1792]{2,1,0:T(8,128)(2,1)S(1)}, u32[]{:S(2)}, u32[]{:S(2)}) collective-permute-start(bf16[2,16,1792]{2,1,0:T(8,128)(2,1)S(1)} %get-tuple-element.46), channel_id=1, source_target_pairs={{0,1},{1,0},{2,3},{3,2},{4,5},{5,4},{6,7},{7,6},{8,9},{9,8},{10,11... | collective-permute-start | bytes 344072 | tf_op jit(solution)/shard_map/ppermute | solution.py:67
  79.5 12.1 %collective-permute-start.14 = (bf16[2,2,16,1536]{3,2,1,0:T(8,128)(2,1)S(1)}, bf16[2,2,16,1536]{3,2,1,0:T(8,128)(2,1)S(1)}, u32[]{:S(2)}, u32[]{:S(2)}) collective-permute-start(bf16[2,2,16,1536]{3,2,1,0:T(8,128)(2,1)S(1)} %get-tuple-element.38), channel_id=1, source_target_pairs={{0,4},{1,5},{2,6},{3,7},{4,0},{5,1},{6,2},{7,3},{8,12},{9,13},{10,... | collective-permute-start | bytes 589832 | tf_op jit(solution)/shard_map/ppermute | solution.py:67
  81.3 7.2 %collective-permute-start.3 = (bf16[2,2,16,1792]{3,2,1,0:T(8,128)(2,1)S(1)}, bf16[2,2,16,1792]{3,2,1,0:T(8,128)(2,1)S(1)}, u32[]{:S(2)}, u32[]{:S(2)}) collective-permute-start(bf16[2,2,16,1792]{3,2,1,0:T(8,128)(2,1)S(1)} %get-tuple-element.36), channel_id=1, source_target_pairs={{0,1},{1,0},{2,3},{3,2},{4,5},{5,4},{6,7},{7,6},{8,9},{9,8},{10,11... | collective-permute-start | bytes 688136 | tf_op jit(solution)/shard_map/ppermute | solution.py:67
  82.9 7.2 %collective-permute-start.9 = (bf16[2,2,16,1792]{3,2,1,0:T(8,128)(2,1)S(1)}, bf16[2,2,16,1792]{3,2,1,0:T(8,128)(2,1)S(1)}, u32[]{:S(2)}, u32[]{:S(2)}) collective-permute-start(bf16[2,2,16,1792]{3,2,1,0:T(8,128)(2,1)S(1)} %get-tuple-element.34), channel_id=1, source_target_pairs={{0,32},{1,33},{2,34},{3,35},{4,36},{5,37},{6,38},{7,39},{8,40},{9,... | collective-permute-start | bytes 688136 | tf_op jit(solution)/shard_map/ppermute | solution.py:67
  88.6 11.1 %collective-permute-start.4 = (bf16[2,2,2,16,1792]{4,3,2,1,0:T(8,128)(2,1)S(1)}, bf16[2,2,2,16,1792]{4,3,2,1,0:T(8,128)(2,1)S(1)}, u32[]{:S(2)}, u32[]{:S(2)}) collective-permute-start(bf16[2,2,2,16,1792]{4,3,2,1,0:T(8,128)(2,1)S(1)} %get-tuple-element.28), channel_id=1, source_target_pairs={{0,16},{1,17},{2,18},{3,19},{4,20},{5,21},{6,22},{7,23},{8,56},{9,... | collective-permute-start | bytes 1376264 | tf_op jit(solution)/shard_map/ppermute | solution.py:67
  90.1 10.9 %collective-permute-start.10 = (bf16[2,2,2,16,1792]{4,3,2,1,0:T(8,128)(2,1)S(1)}, bf16[2,2,2,16,1792]{4,3,2,1,0:T(8,128)(2,1)S(1)}, u32[]{:S(2)}, u32[]{:S(2)}) collective-permute-start(bf16[2,2,2,16,1792]{4,3,2,1,0:T(8,128)(2,1)S(1)} %get-tuple-element.26), channel_id=1, source_target_pairs={{0,2},{1,3},{2,0},{3,1},{4,6},{5,7},{6,4},{7,5},{8,14},{9,15},{10,... | collective-permute-start | bytes 1376264 | tf_op jit(solution)/shard_map/ppermute | solution.py:67
  91.7 10.7 %collective-permute-start.15 = (bf16[2,2,2,16,1536]{4,3,2,1,0:T(8,128)(2,1)S(1)}, bf16[2,2,2,16,1536]{4,3,2,1,0:T(8,128)(2,1)S(1)}, u32[]{:S(2)}, u32[]{:S(2)}) collective-permute-start(bf16[2,2,2,16,1536]{4,3,2,1,0:T(8,128)(2,1)S(1)} %get-tuple-element.30), channel_id=1, source_target_pairs={{0,64},{1,65},{2,66},{3,67},{4,68},{5,69},{6,70},{7,71},{8,73},{9,... | collective-permute-start | bytes 1179656 | tf_op jit(solution)/shard_map/ppermute | solution.py:67
  99.8 15.9 %collective-permute-start.6 = (bf16[2,2,2,2,16,1792]{5,4,3,2,1,0:T(8,128)(2,1)S(1)}, bf16[2,2,2,2,16,1792]{5,4,3,2,1,0:T(8,128)(2,1)S(1)}, u32[]{:S(2)}, u32[]{:S(2)}) collective-permute-start(bf16[2,2,2,2,16,1792]{5,4,3,2,1,0:T(8,128)(2,1)S(1)} %pad_maximum_fusion.1.refs_0_), channel_id=1, source_target_pairs={{0,2},{1,3},{2,0},{3,1},{4,6},{5,7},{6,4},{7,5},{8,14},{9,15},{10,... | collective-permute-start | bytes 2752520 | tf_op jit(solution)/shard_map/ppermute | solution.py:67
  101.1 14.6 %collective-permute-start.11 = (bf16[2,2,2,2,16,1792]{5,4,3,2,1,0:T(8,128)(2,1)S(1)}, bf16[2,2,2,2,16,1792]{5,4,3,2,1,0:T(8,128)(2,1)}, u32[]{:S(2)}, u32[]{:S(2)}) collective-permute-start(bf16[2,2,2,2,16,1792]{5,4,3,2,1,0:T(8,128)(2,1)S(1)} %pad_maximum_fusion.2.refs_2_), channel_id=1, source_target_pairs={{0,64},{1,65},{2,66},{3,67},{4,68},{5,69},{6,70},{7,71},{8,73},{9,... | collective-permute-start | bytes 2752520 | tf_op jit(solution)/shard_map/ppermute | solution.py:67
  102.5 12.3 %collective-permute-start.16 = (bf16[2,2,2,2,16,1536]{5,4,3,2,1,0:T(8,128)(2,1)S(1)}, bf16[2,2,2,2,16,1536]{5,4,3,2,1,0:T(8,128)(2,1)S(1)}, u32[]{:S(2)}, u32[]{:S(2)}) collective-permute-start(bf16[2,2,2,2,16,1536]{5,4,3,2,1,0:T(8,128)(2,1)S(1)} %pad_maximum_fusion.3.refs_4_), channel_id=1, source_target_pairs={{0,16},{1,17},{2,18},{3,19},{4,20},{5,21},{6,22},{7,23},{8,56},{9,... | collective-permute-start | bytes 2359304 | tf_op jit(solution)/shard_map/ppermute | solution.py:67
  103.7 18.2 %collective-permute-start.20 = (bf16[2,2,2,2,16,1536]{5,4,3,2,1,0:T(8,128)(2,1)S(1)}, bf16[2,2,2,2,16,1536]{5,4,3,2,1,0:T(8,128)(2,1)}, u32[]{:S(2)}, u32[]{:S(2)}) collective-permute-start(bf16[2,2,2,2,16,1536]{5,4,3,2,1,0:T(8,128)(2,1)S(1)} %pad_maximum_fusion.3.refs_4_), channel_id=1, source_target_pairs={{0,2},{1,3},{2,0},{3,1},{4,6},{5,7},{6,4},{7,5},{8,14},{9,15},{10,... | collective-permute-start | bytes 2359304 | tf_op jit(solution)/shard_map/ppermute | solution.py:67
  106.1 32.5 %collective-permute-start.5 = (bf16[2,2,2,2,16,1792]{5,4,3,2,1,0:T(8,128)(2,1)S(1)}, bf16[2,2,2,2,16,1792]{5,4,3,2,1,0:T(8,128)(2,1)}, u32[]{:S(2)}, u32[]{:S(2)}) collective-permute-start(bf16[2,2,2,2,16,1792]{5,4,3,2,1,0:T(8,128)(2,1)S(1)} %pad_maximum_fusion.1.refs_0_), channel_id=1, source_target_pairs={{0,64},{1,65},{2,66},{3,67},{4,68},{5,69},{6,70},{7,71},{8,73},{9,... | collective-permute-start | bytes 2752520 | tf_op jit(solution)/shard_map/ppermute | solution.py:67
  114.8 1.0 copy-start.2
  114.8 23.9 %collective-permute-start.18 = (bf16[2,2,2,2,16,1792]{5,4,3,2,1,0:T(8,128)(2,1)S(1)}, bf16[2,2,2,2,16,1792]{5,4,3,2,1,0:T(8,128)(2,1)}, u32[]{:S(2)}, u32[]{:S(2)}) collective-permute-start(bf16[2,2,2,2,16,1792]{5,4,3,2,1,0:T(8,128)(2,1)S(1)} %pad_maximum_fusion.2.refs_2_), channel_id=1, source_target_pairs={{0,16},{1,17},{2,18},{3,19},{4,20},{5,21},{6,22},{7,23},{8,56},{9,... | collective-permute-start | bytes 2752520 | tf_op jit(solution)/shard_map/ppermute | solution.py:67
  115.8 23.0 %collective-permute-start.17 = (bf16[2,2,2,2,16,1792]{5,4,3,2,1,0:T(8,128)(2,1)S(1)}, bf16[2,2,2,2,16,1792]{5,4,3,2,1,0:T(8,128)(2,1)}, u32[]{:S(2)}, u32[]{:S(2)}) collective-permute-start(bf16[2,2,2,2,16,1792]{5,4,3,2,1,0:T(8,128)(2,1)S(1)} %collective-permute-done.6.refs_1_), channel_id=1, source_target_pairs={{0,64},{1,65},{2,66},{3,67},{4,68},{5,69},{6,70},{7,71},{8,73},{9,... | collective-permute-start | bytes 2752520 | tf_op jit(solution)/shard_map/ppermute | solution.py:67
  117.5 21.3 %collective-permute-start.19 = (bf16[2,2,2,2,16,1792]{5,4,3,2,1,0:T(8,128)(2,1)}, bf16[2,2,2,2,16,1792]{5,4,3,2,1,0:T(8,128)(2,1)}, u32[]{:S(2)}, u32[]{:S(2)}) collective-permute-start(bf16[2,2,2,2,16,1792]{5,4,3,2,1,0:T(8,128)(2,1)} %collective-permute-done.11.refs_3_), channel_id=1, source_target_pairs={{0,16},{1,17},{2,18},{3,19},{4,20},{5,21},{6,22},{7,23},{8,56},{9,... | collective-permute-start | bytes 2752520 | tf_op jit(solution)/shard_map/ppermute | solution.py:67
  121.9 16.8 %collective-permute-start.21 = (bf16[2,2,2,2,16,1536]{5,4,3,2,1,0:T(8,128)(2,1)}, bf16[2,2,2,2,16,1536]{5,4,3,2,1,0:T(8,128)(2,1)}, u32[]{:S(2)}, u32[]{:S(2)}) collective-permute-start(bf16[2,2,2,2,16,1536]{5,4,3,2,1,0:T(8,128)(2,1)} %copy-done.2), channel_id=1, source_target_pairs={{0,2},{1,3},{2,0},{3,1},{4,6},{5,7},{6,4},{7,5},{8,14},{9,15},{10,... | collective-permute-start | bytes 2359304 | tf_op jit(solution)/shard_map/ppermute | solution.py:67
  123.1 1.1 copy-start.3
  138.7 24.7 %copy-start.6 = (s32[32]{0:T(128)S(1)}, s32[32]{0:T(128)}, u32[]{:S(2)}) copy-start(s32[32]{0:T(128)} %get-tuple-element.22) | copy-start | bytes 388
  153.8 28.9 %collective-permute-start.22 = (f32[2,2,2,8,16,640]{5,4,3,2,1,0:T(8,128)}, f32[2,2,2,8,16,640]{5,4,3,2,1,0:T(8,128)}, u32[]{:S(2)}, u32[]{:S(2)}) collective-permute-start(f32[2,2,2,8,16,640]{5,4,3,2,1,0:T(8,128)} %get-tuple-element.24), channel_id=1, source_target_pairs={{0,8},{1,9},{2,10},{3,11},{4,12},{5,13},{6,14},{7,15},{8,0},{9,1},... | collective-permute-start | bytes 7864328 | tf_op jit(solution)/shard_map/ppermute | solution.py:58
  158.9 11.1 %all-to-all-start.2 = ((f32[8,1,1024]{2,1,0:T(1,128)}), f32[8,1,1024]{2,1,0:T(1,128)S(1)}, u32[]{:S(2)}, u32[]{:S(2)}) async-start(f32[8,1,1024]{2,1,0:T(1,128)} %broadcast_in_dim.16), calls=%async_computation.2 | async-start | bytes 65536 | tf_op jit(solution)/shard_map/all_to_all | solution.py:371
  170.7 10.6 %all-to-all-start.3 = ((f32[16,1,1056]{2,1,0:T(1,128)}), f32[16,1,1056]{2,1,0:T(1,128)S(1)}, u32[]{:S(2)}, u32[]{:S(2)}) async-start(f32[16,1,1056]{2,1,0:T(1,128)} %broadcast_in_dim.17), calls=%async_computation.3 | async-start | bytes 147456 | tf_op jit(solution)/shard_map/all_to_all | solution.py:371
  (1 other events, 0.7 us)
where the time goes:
time: 191 us; the launch traced here: 190 us
  starting transfers between devices  51 us (27%)
  Pallas kernels  47.5 us (25%)
  waiting for transfers between devices  42.8 us (22%)
  blocking collectives  38.8 us (20%)
  local copies, waits for them, and re-layouts  4.98 us (3%)
  matrix products  2.76 us (1%)
  other arithmetic  2.09 us (1%)
    all_to_all x1, blocking collectives, on_device(): arrived = lax.all_to_all(both, 'vocab', 0, 0, tiled=True)  38.8 us
    ppermute x21, starting transfers between devices, meet(): lax.ppermute(part, BOTH, pairs[order[turn % 3]])  31.5 us
    pallas_call x2, Pallas kernels, call(): pl.pallas_call(functools.partial(head_kernel, mark), out_shape=out_shape,...  29.5 us
    ppermute x21, waiting for transfers between devices, meet(): lax.ppermute(part, BOTH, pairs[order[turn % 3]])  22.5 us
    all_to_all x2, waiting for transfers between devices, spread(): lax.all_to_all(jnp.broadcast_to(values[None], (copies,) + values.shape),...  12.4 us
    all_to_all x2, starting transfers between devices, spread(): lax.all_to_all(jnp.broadcast_to(values[None], (copies,) + values.shape),...  9.23 us
    all_to_all x1, waiting for transfers between devices, on_device(): local = lax.all_to_all(sorted_rows, 'grp', 0, 0, tiled=True)  7.95 us
    pallas_call x1, Pallas kernels, ordered_output(): pl.pallas_call(output_kernel, out_shape=jax.ShapeDtypeStruct((512, 4, wid...  7.68 us
  transfers between devices with their start and end apart: 26, of which 9 were waited for; matrix products, arithmetic and copies ran while one was open for 3% of the time, Pallas kernels for 13%

commit v1 on v0

--- a/solution.py
+++ b/solution.py
@@ -9,7 +9,7 @@
 
 BOTH = ("grp", "vocab")
 RING = 4
-PIECES = ((0, 1792), (1792, 3584), (3584, 5120))
+PIECES = ((0, 1536), (1536, 3328), (3328, 5120))
 ORDERS = ("xyz", "yzx", "zxy")
 
 

time: 191 us -> 190 us (level)
  starting transfers between devices: 51 us -> 45.6 us
  waiting for transfers between devices: 42.8 us -> 48 us
  Pallas kernels: 47.5 us -> 45.4 us
    ppermute x21, waiting for transfers between devices: 22.5 us -> 27.7 us  [meet(): lax.ppermute(part, BOTH, pairs[order[turn % 3]])]
    ppermute x21, starting transfers between devices: 31.5 us -> 27.1 us  [meet(): lax.ppermute(part, BOTH, pairs[order[turn % 3]])]
    pallas_call x2, Pallas kernels: 29.5 us -> 27.5 us  [call(): pl.pallas_call(functools.partial(head_kernel, mark), out_shape=out_shape,...]
  transfers between devices with their start and end apart: 26 -> 26, of which waited for: 9 -> 12; matrix products, arithmetic and copies ran while one was open for 3% -> 3% of each run, Pallas kernels for 13% -> 12%
where the time goes in v1:
time: 190 us; the launch traced here: 189 us
  waiting for transfers between devices  48 us (25%)
  starting transfers between devices  45.6 us (24%)
  Pallas kernels  45.4 us (24%)
  blocking collectives  38.8 us (20%)
  local copies, waits for them, and re-layouts  5.9 us (3%)
  matrix products  2.76 us (1%)
  other arithmetic  2.09 us (1%)
    all_to_all x1, blocking collectives, on_device(): arrived = lax.all_to_all(both, 'vocab', 0, 0, tiled=True)  38.8 us
    ppermute x21, waiting for transfers between devices, meet(): lax.ppermute(part, BOTH, pairs[order[turn % 3]])  27.7 us
    pallas_call x2, Pallas kernels, call(): pl.pallas_call(functools.partial(head_kernel, mark), out_shape=out_shape,...  27.5 us
    ppermute x21, starting transfers between devices, meet(): lax.ppermute(part, BOTH, pairs[order[turn % 3]])  27.1 us
    all_to_all x2, waiting for transfers between devices, spread(): lax.all_to_all(jnp.broadcast_to(values[None], (copies,) + values.shape),...  12.3 us
    all_to_all x2, starting transfers between devices, spread(): lax.all_to_all(jnp.broadcast_to(values[None], (copies,) + values.shape),...  9.27 us
    all_to_all x1, waiting for transfers between devices, on_device(): local = lax.all_to_all(sorted_rows, 'grp', 0, 0, tiled=True)  7.95 us
    pallas_call x1, Pallas kernels, ordered_output(): pl.pallas_call(output_kernel, out_shape=jax.ShapeDtypeStruct((512, 4, wid...  7.68 us
  transfers between devices with their start and end apart: 26, of which 12 were waited for; matrix products, arithmetic and copies ran while one was open for 3% of the time, Pallas kernels for 12%

profile of v1, /device:TPU:1, one launch (start us, length us, event | category | flops | bytes accessed | tf_op | source)
XLA Modules:
  0.0 189.0 jit_solution(10490394509178180216)
XLA Ops:
  0.0 1.4 collective-permute-start
  1.4 7.1 %front.1 = (bf16[128,1408]{1,0:T(8,128)(2,1)}, s32[32]{0:T(128)}) custom-call(s32[32]{0:T(128)} %prompts.1, s32[1]{0:T(128)} %bitcast.column, bf16[32,4,5120]{2,1,0:T(4,128)(2,1)} %embedded.1, f32[1,5120]{1,0:T(1,128)} %bitcast.84, bf16[5120,512]{1,0:T(8,128)(2,1)} %query_w.1, bf16[5120,128]{1,0:T(8,128)(2,1)} %key_w.1, bf16[5120,128]{1,0:T(8,128)(2,1)} %value_w.1), custom_call_target="tpu_custom_call" | custom-call | flops 1006632960 | bytes 10000000 | tf_op jit(solution)/shard_map/front/pallas_call | solution.py:254
  8.6 5.9 %all-to-all-start = ((bf16[16,8,1408]{2,1,0:T(8,128)(2,1)}), bf16[16,8,1408]{2,1,0:T(8,128)(2,1)S(1)}, u32[]{:S(2)}, u32[]{:S(2)}) async-start(bf16[16,8,1408]{2,1,0:T(8,128)(2,1)} %bitcast.70), calls=%async_computation | async-start | bytes 720896 | tf_op jit(solution)/shard_map/all_to_all | solution.py:414
  14.4 7.9 %all-to-all-done = bf16[16,8,1408]{2,1,0:T(8,128)(2,1)S(1)} async-done(((bf16[16,8,1408]{2,1,0:T(8,128)(2,1)}), bf16[16,8,1408]{2,1,0:T(8,128)(2,1)S(1)}, u32[]{:S(2)}, u32[]{:S(2)}) %all-to-all-start) | async-done | bytes 360480 | tf_op jit(solution)/shard_map/all_to_all | solution.py:414
  22.4 3.2 %attend.1 = bf16[128,512]{1,0:T(8,128)(2,1)S(1)} custom-call(bf16[128,1408]{1,0:T(8,128)(2,1)S(1)} %bitcast.62, bf16[2048,128]{1,0:T(8,128)(2,1)S(1)} %bitcast.64, bf16[2048,128]{1,0:T(8,128)(2,1)S(1)} %bitcast.65), custom_call_target="tpu_custom_call" | custom-call | tf_op jit(solution)/shard_map/attend/pallas_call | solution.py:313
  25.6 2.2 %fusion.2 = f32[128,2560]{1,0:T(8,128)S(1)} fusion(bf16[128,512]{1,0:T(8,128)(2,1)S(1)} %attend.1, bf16[512,5120]{1,0:T(8,128)(2,1)} %param.16), kind=kOutput, calls=%fused_computation.4 | convolution fusion | flops 335544320 | bytes 4063232 | tf_op jit(solution)/shard_map/dot_general | solution.py:422
  28.7 38.8 %all_to_all.38 = f32[8,16,5120]{2,1,0:T(8,128)S(1)} all-to-all(f32[8,16,5120]{2,1,0:T(8,128)S(1)} %bitcast.66), channel_id=1, replica_groups=mesh['grp'=16,'vocab'=8] {'vocab'}, dimensions={0} | all-to-all | bytes 5242880 | tf_op jit(solution)/shard_map/all_to_all | solution.py:429
  68.4 3.1 %collective-permute-start.1 = (bf16[16,1536]{1,0:T(8,128)(2,1)S(1)}, bf16[16,1536]{1,0:T(8,128)(2,1)S(1)}, u32[]{:S(2)}, u32[]{:S(2)}) collective-permute-start(bf16[16,1536]{1,0:T(8,128)(2,1)S(1)} %get-tuple-element.44), channel_id=1, source_target_pairs={{0,32},{1,33},{2,34},{3,35},{4,36},{5,37},{6,38},{7,39},{8,40},{9,... | collective-permute-start | bytes 147464 | tf_op jit(solution)/shard_map/ppermute | solution.py:67
  73.3 2.5 %collective-permute-start.2 = (bf16[2,16,1536]{2,1,0:T(8,128)(2,1)S(1)}, bf16[2,16,1536]{2,1,0:T(8,128)(2,1)S(1)}, u32[]{:S(2)}, u32[]{:S(2)}) collective-permute-start(bf16[2,16,1536]{2,1,0:T(8,128)(2,1)S(1)} %get-tuple-element.50), channel_id=1, source_target_pairs={{0,4},{1,5},{2,6},{3,7},{4,0},{5,1},{6,2},{7,3},{8,12},{9,13},{10,... | collective-permute-start | bytes 294920 | tf_op jit(solution)/shard_map/ppermute | solution.py:67
  76.4 1.3 collective-permute-start.8
  79.1 1.6 collective-permute-start.3
  83.0 1.5 collective-permute-start.14
  84.5 4.3 %collective-permute-done.9 = bf16[2,2,16,1792]{3,2,1,0:T(8,128)(2,1)S(1)} collective-permute-done((bf16[2,2,16,1792]{3,2,1,0:T(8,128)(2,1)S(1)}, bf16[2,2,16,1792]{3,2,1,0:T(8,128)(2,1)S(1)}, u32[]{:S(2)}, u32[]{:S(2)}) %collective-permute-start.9) | collective-permute-done | bytes 229408 | tf_op jit(solution)/shard_map/ppermute | solution.py:67
  91.2 1.4 collective-permute-start.4
  92.6 7.1 %collective-permute-done.10 = bf16[2,2,2,16,1792]{4,3,2,1,0:T(8,128)(2,1)S(1)} collective-permute-done((bf16[2,2,2,16,1792]{4,3,2,1,0:T(8,128)(2,1)S(1)}, bf16[2,2,2,16,1792]{4,3,2,1,0:T(8,128)(2,1)S(1)}, u32[]{:S(2)}, u32[]{:S(2)}) %collective-permute-start.10) | collective-permute-done | bytes 458784 | tf_op jit(solution)/shard_map/ppermute | solution.py:67
  99.9 1.4 collective-permute-start.11
  101.3 2.1 %collective-permute-start.16 = (bf16[2,2,2,2,16,1792]{5,4,3,2,1,0:T(8,128)(2,1)S(1)}, bf16[2,2,2,2,16,1792]{5,4,3,2,1,0:T(8,128)(2,1)}, u32[]{:S(2)}, u32[]{:S(2)}) collective-permute-start(bf16[2,2,2,2,16,1792]{5,4,3,2,1,0:T(8,128)(2,1)S(1)} %pad_maximum_fusion.2.refs_4_), channel_id=1, source_target_pairs={{0,16},{1,17},{2,18},{3,19},{4,20},{5,21},{6,22},{7,23},{8,56},{9,... | collective-permute-start | bytes 2752520 | tf_op jit(solution)/shard_map/ppermute | solution.py:67
  103.7 1.6 collective-permute-start.5
  105.4 1.5 collective-permute-start.18
  106.9 8.9 %collective-permute-done.6.refs_1_ = bf16[2,2,2,2,16,1536]{5,4,3,2,1,0:T(8,128)(2,1)S(1)} collective-permute-done((bf16[2,2,2,2,16,1536]{5,4,3,2,1,0:T(8,128)(2,1)S(1)}, bf16[2,2,2,2,16,1536]{5,4,3,2,1,0:T(8,128)(2,1)S(1)}, u32[]{:S(2)}, u32[]{:S(2)}) %collective-permute-start.6) | collective-permute-done | bytes 786464 | tf_op jit(solution)/shard_map/ppermute | solution.py:67
  117.5 1.7 collective-permute-start.21
  119.3 2.7 %collective-permute-done.5.refs_0_ = bf16[2,2,2,2,16,1536]{5,4,3,2,1,0:T(8,128)(2,1)} collective-permute-done((bf16[2,2,2,2,16,1536]{5,4,3,2,1,0:T(8,128)(2,1)S(1)}, bf16[2,2,2,2,16,1536]{5,4,3,2,1,0:T(8,128)(2,1)}, u32[]{:S(2)}, u32[]{:S(2)}) %collective-permute-start.5) | collective-permute-done | bytes 786464 | tf_op jit(solution)/shard_map/ppermute | solution.py:67
  121.9 1.3 collective-permute-start.17
  124.4 13.0 %head_early.1.refs_8_ = f32[2,2,2,8,16,1280]{5,4,3,2,1,0:T(8,128)} custom-call(bf16[2,2,2,2,16,1536]{5,4,3,2,1,0:T(8,128)(2,1)S(1)} %pad_maximum_fusion.3.refs_0_, bf16[2,2,2,2,16,1536]{5,4,3,2,1,0:T(8,128)(2,1)S(1)} %copy-done.3, bf16[2,2,2,2,16,1792]{5,4,3,2,1,0:T(8,128)(2,1)S(1)} %pad_maximum_fusion.1.refs_2_, ...), custom_call_target="tpu_custom_call" | custom-call | flops 6710886400 | bytes 26000000 | tf_op jit(solution)/shard_map/head_early/pallas_call | solution.py:176
  137.5 1.6 collective-permute-done.21.refs_5_
  139.2 14.4 %head_late.1 = (f32[2,2,2,8,16,640]{5,4,3,2,1,0:T(8,128)}, f32[2,2,2,8,16,640]{5,4,3,2,1,0:T(8,128)}, f32[1024,1]{1,0:T(8,128)S(1)}) custom-call(bf16[2,2,2,2,16,1536]{5,4,3,2,1,0:T(8,128)(2,1)} %collective-permute-done.5.refs_0_, bf16[2,2,2,2,16,1536]{5,4,3,2,1,0:T(8,128)(2,1)} %collective-permute-done.17.refs_1_, ...), custom_call_target="tpu_custom_call" | custom-call | flops 6710886400 | bytes 26000000 | tf_op jit(solution)/shard_map/head_late/pallas_call | solution.py:176
  153.6 1.9 collective-permute-start.22
  157.6 3.9 %all-to-all-start.2 = ((f32[8,1,1024]{2,1,0:T(1,128)}), f32[8,1,1024]{2,1,0:T(1,128)S(1)}, u32[]{:S(2)}, u32[]{:S(2)}) async-start(f32[8,1,1024]{2,1,0:T(1,128)} %broadcast_in_dim.16), calls=%async_computation.2 | async-start | bytes 65536 | tf_op jit(solution)/shard_map/all_to_all | solution.py:371
  161.5 6.6 %all-to-all-done.2 = f32[8,1,1024]{2,1,0:T(1,128)S(1)} async-done(((f32[8,1,1024]{2,1,0:T(1,128)}), f32[8,1,1024]{2,1,0:T(1,128)S(1)}, u32[]{:S(2)}, u32[]{:S(2)}) %all-to-all-start.2) | async-done | bytes 32800 | tf_op jit(solution)/shard_map/all_to_all | solution.py:371
  168.9 5.4 %all-to-all-start.3 = ((f32[16,1,1056]{2,1,0:T(1,128)}), f32[16,1,1056]{2,1,0:T(1,128)S(1)}, u32[]{:S(2)}, u32[]{:S(2)}) async-start(f32[16,1,1056]{2,1,0:T(1,128)} %broadcast_in_dim.17), calls=%async_computation.3 | async-start | bytes 147456 | tf_op jit(solution)/shard_map/all_to_all | solution.py:371
  174.3 5.8 %all-to-all-done.3 = f32[16,1,1056]{2,1,0:T(1,128)S(1)} async-done(((f32[16,1,1056]{2,1,0:T(1,128)}), f32[16,1,1056]{2,1,0:T(1,128)S(1)}, u32[]{:S(2)}, u32[]{:S(2)}) %all-to-all-start.3) | async-done | bytes 67616 | tf_op jit(solution)/shard_map/all_to_all | solution.py:371
  181.3 7.7 %output.1 = f32[512,4,640]{2,1,0:T(4,128)} custom-call(s32[512]{0:T(512)S(1)} %reshape.282.order, s32[4]{0:T(128)S(1)} %pad_add_fusion.place, f32[2,2,2,8,16,640]{5,4,3,2,1,0:T(8,128)} %get-tuple-element.23.own, f32[2,2,2,8,16,640]{5,4,3,2,1,0:T(8,128)} %collective-permute-done.22.other, f32[16,8,16,1]{3,2,1,0:T(8,128)S(1)} %copy.24.totals), custom_call_target="tpu_custom_call" | custom-call | tf_op jit(solution)/shard_map/output/pallas_call | solution.py:345
  (97 shorter events, 17.8 us)
Async XLA Ops:
  0.0 25.6 %collective-permute-start = (bf16[5120,640]{1,0:T(8,128)(2,1)}, bf16[5120,640]{1,0:T(8,128)(2,1)}, u32[]{:S(2)}, u32[]{:S(2)}) collective-permute-start(bf16[5120,640]{1,0:T(8,128)(2,1)} %refs_6_.3), channel_id=1, source_target_pairs={{0,8},{1,9},{2,10},{3,11},{4,12},{5,13},{6,14},{7,15},{8,0},{9,1},... | collective-permute-start | bytes 19660808 | tf_op jit(solution)/shard_map/ppermute | solution.py:58
  1.4 21.0 %copy-start = (bf16[1,1,2048,128]{3,2,1,0:T(8,128)(2,1)S(1)}, bf16[1,1,2048,128]{3,2,1,0:T(8,128)(2,1)}, u32[]{:S(2)}) copy-start(bf16[1,1,2048,128]{3,2,1,0:T(8,128)(2,1)} %param.19) | copy-start | bytes 1572868
  1.4 21.0 %copy-start.1 = (bf16[1,1,2048,128]{3,2,1,0:T(8,128)(2,1)S(1)}, bf16[1,1,2048,128]{3,2,1,0:T(8,128)(2,1)}, u32[]{:S(2)}) copy-start(bf16[1,1,2048,128]{3,2,1,0:T(8,128)(2,1)} %param.20) | copy-start | bytes 1572868
  8.6 13.8 %all-to-all-start = ((bf16[16,8,1408]{2,1,0:T(8,128)(2,1)}), bf16[16,8,1408]{2,1,0:T(8,128)(2,1)S(1)}, u32[]{:S(2)}, u32[]{:S(2)}) async-start(bf16[16,8,1408]{2,1,0:T(8,128)(2,1)} %bitcast.70), calls=%async_computation | async-start | bytes 720896 | tf_op jit(solution)/shard_map/all_to_all | solution.py:414
  22.4 5.5 %copy-start.4 = (bf16[512,5120]{1,0:T(8,128)(2,1)S(1)}, bf16[512,5120]{1,0:T(8,128)(2,1)}, u32[]{:S(2)}) copy-start(bf16[512,5120]{1,0:T(8,128)(2,1)} %param.16) | copy-start | bytes 15728644
  68.4 4.9 %collective-permute-start.1 = (bf16[16,1536]{1,0:T(8,128)(2,1)S(1)}, bf16[16,1536]{1,0:T(8,128)(2,1)S(1)}, u32[]{:S(2)}, u32[]{:S(2)}) collective-permute-start(bf16[16,1536]{1,0:T(8,128)(2,1)S(1)} %get-tuple-element.44), channel_id=1, source_target_pairs={{0,32},{1,33},{2,34},{3,35},{4,36},{5,37},{6,38},{7,39},{8,40},{9,... | collective-permute-start | bytes 147464 | tf_op jit(solution)/shard_map/ppermute | solution.py:67
  71.5 4.9 %collective-permute-start.7 = (bf16[16,1792]{1,0:T(8,128)(2,1)S(1)}, bf16[16,1792]{1,0:T(8,128)(2,1)S(1)}, u32[]{:S(2)}, u32[]{:S(2)}) collective-permute-start(bf16[16,1792]{1,0:T(8,128)(2,1)S(1)} %get-tuple-element.42), channel_id=1, source_target_pairs={{0,4},{1,5},{2,6},{3,7},{4,0},{5,1},{6,2},{7,3},{8,12},{9,13},{10,... | collective-permute-start | bytes 172040 | tf_op jit(solution)/shard_map/ppermute | solution.py:67
  72.6 5.1 %collective-permute-start.12 = (bf16[16,1792]{1,0:T(8,128)(2,1)S(1)}, bf16[16,1792]{1,0:T(8,128)(2,1)S(1)}, u32[]{:S(2)}, u32[]{:S(2)}) collective-permute-start(bf16[16,1792]{1,0:T(8,128)(2,1)S(1)} %get-tuple-element.41), channel_id=1, source_target_pairs={{0,1},{1,0},{2,3},{3,2},{4,5},{5,4},{6,7},{7,6},{8,9},{9,8},{10,11... | collective-permute-start | bytes 172040 | tf_op jit(solution)/shard_map/ppermute | solution.py:67
  73.3 5.8 %collective-permute-start.2 = (bf16[2,16,1536]{2,1,0:T(8,128)(2,1)S(1)}, bf16[2,16,1536]{2,1,0:T(8,128)(2,1)S(1)}, u32[]{:S(2)}, u32[]{:S(2)}) collective-permute-start(bf16[2,16,1536]{2,1,0:T(8,128)(2,1)S(1)} %get-tuple-element.50), channel_id=1, source_target_pairs={{0,4},{1,5},{2,6},{3,7},{4,0},{5,1},{6,2},{7,3},{8,12},{9,13},{10,... | collective-permute-start | bytes 294920 | tf_op jit(solution)/shard_map/ppermute | solution.py:67
  76.4 5.5 %collective-permute-start.8 = (bf16[2,16,1792]{2,1,0:T(8,128)(2,1)S(1)}, bf16[2,16,1792]{2,1,0:T(8,128)(2,1)S(1)}, u32[]{:S(2)}, u32[]{:S(2)}) collective-permute-start(bf16[2,16,1792]{2,1,0:T(8,128)(2,1)S(1)} %get-tuple-element.48), channel_id=1, source_target_pairs={{0,1},{1,0},{2,3},{3,2},{4,5},{5,4},{6,7},{7,6},{8,9},{9,8},{10,11... | collective-permute-start | bytes 344072 | tf_op jit(solution)/shard_map/ppermute | solution.py:67
  77.8 5.2 %collective-permute-start.13 = (bf16[2,16,1792]{2,1,0:T(8,128)(2,1)S(1)}, bf16[2,16,1792]{2,1,0:T(8,128)(2,1)S(1)}, u32[]{:S(2)}, u32[]{:S(2)}) collective-permute-start(bf16[2,16,1792]{2,1,0:T(8,128)(2,1)S(1)} %get-tuple-element.46), channel_id=1, source_target_pairs={{0,32},{1,33},{2,34},{3,35},{4,36},{5,37},{6,38},{7,39},{8,40},{9,... | collective-permute-start | bytes 344072 | tf_op jit(solution)/shard_map/ppermute | solution.py:67
  79.1 12.0 %collective-permute-start.3 = (bf16[2,2,16,1536]{3,2,1,0:T(8,128)(2,1)S(1)}, bf16[2,2,16,1536]{3,2,1,0:T(8,128)(2,1)S(1)}, u32[]{:S(2)}, u32[]{:S(2)}) collective-permute-start(bf16[2,2,16,1536]{3,2,1,0:T(8,128)(2,1)S(1)} %get-tuple-element.38), channel_id=1, source_target_pairs={{0,1},{1,0},{2,3},{3,2},{4,5},{5,4},{6,7},{7,6},{8,9},{9,8},{10,11... | collective-permute-start | bytes 589832 | tf_op jit(solution)/shard_map/ppermute | solution.py:67
  82.0 6.8 %collective-permute-start.9 = (bf16[2,2,16,1792]{3,2,1,0:T(8,128)(2,1)S(1)}, bf16[2,2,16,1792]{3,2,1,0:T(8,128)(2,1)S(1)}, u32[]{:S(2)}, u32[]{:S(2)}) collective-permute-start(bf16[2,2,16,1792]{3,2,1,0:T(8,128)(2,1)S(1)} %get-tuple-element.36), channel_id=1, source_target_pairs={{0,32},{1,33},{2,34},{3,35},{4,36},{5,37},{6,38},{7,39},{8,40},{9,... | collective-permute-start | bytes 688136 | tf_op jit(solution)/shard_map/ppermute | solution.py:67
  83.0 6.8 %collective-permute-start.14 = (bf16[2,2,16,1792]{3,2,1,0:T(8,128)(2,1)S(1)}, bf16[2,2,16,1792]{3,2,1,0:T(8,128)(2,1)S(1)}, u32[]{:S(2)}, u32[]{:S(2)}) collective-permute-start(bf16[2,2,16,1792]{3,2,1,0:T(8,128)(2,1)S(1)} %get-tuple-element.34), channel_id=1, source_target_pairs={{0,4},{1,5},{2,6},{3,7},{4,0},{5,1},{6,2},{7,3},{8,12},{9,13},{10,... | collective-permute-start | bytes 688136 | tf_op jit(solution)/shard_map/ppermute | solution.py:67
  88.8 11.0 %collective-permute-start.10 = (bf16[2,2,2,16,1792]{4,3,2,1,0:T(8,128)(2,1)S(1)}, bf16[2,2,2,16,1792]{4,3,2,1,0:T(8,128)(2,1)S(1)}, u32[]{:S(2)}, u32[]{:S(2)}) collective-permute-start(bf16[2,2,2,16,1792]{4,3,2,1,0:T(8,128)(2,1)S(1)} %get-tuple-element.28), channel_id=1, source_target_pairs={{0,2},{1,3},{2,0},{3,1},{4,6},{5,7},{6,4},{7,5},{8,14},{9,15},{10,... | collective-permute-start | bytes 1376264 | tf_op jit(solution)/shard_map/ppermute | solution.py:67
  89.9 11.3 %collective-permute-start.15 = (bf16[2,2,2,16,1792]{4,3,2,1,0:T(8,128)(2,1)S(1)}, bf16[2,2,2,16,1792]{4,3,2,1,0:T(8,128)(2,1)S(1)}, u32[]{:S(2)}, u32[]{:S(2)}) collective-permute-start(bf16[2,2,2,16,1792]{4,3,2,1,0:T(8,128)(2,1)S(1)} %get-tuple-element.26), channel_id=1, source_target_pairs={{0,64},{1,65},{2,66},{3,67},{4,68},{5,69},{6,70},{7,71},{8,73},{9,... | collective-permute-start | bytes 1376264 | tf_op jit(solution)/shard_map/ppermute | solution.py:67
  91.2 12.1 %collective-permute-start.4 = (bf16[2,2,2,16,1536]{4,3,2,1,0:T(8,128)(2,1)S(1)}, bf16[2,2,2,16,1536]{4,3,2,1,0:T(8,128)(2,1)S(1)}, u32[]{:S(2)}, u32[]{:S(2)}) collective-permute-start(bf16[2,2,2,16,1536]{4,3,2,1,0:T(8,128)(2,1)S(1)} %get-tuple-element.30), channel_id=1, source_target_pairs={{0,16},{1,17},{2,18},{3,19},{4,20},{5,21},{6,22},{7,23},{8,56},{9,... | collective-permute-start | bytes 1179656 | tf_op jit(solution)/shard_map/ppermute | solution.py:67
  99.9 15.9 %collective-permute-start.11 = (bf16[2,2,2,2,16,1792]{5,4,3,2,1,0:T(8,128)(2,1)S(1)}, bf16[2,2,2,2,16,1792]{5,4,3,2,1,0:T(8,128)(2,1)S(1)}, u32[]{:S(2)}, u32[]{:S(2)}) collective-permute-start(bf16[2,2,2,2,16,1792]{5,4,3,2,1,0:T(8,128)(2,1)S(1)} %pad_maximum_fusion.1.refs_2_), channel_id=1, source_target_pairs={{0,64},{1,65},{2,66},{3,67},{4,68},{5,69},{6,70},{7,71},{8,73},{9,... | collective-permute-start | bytes 2752520 | tf_op jit(solution)/shard_map/ppermute | solution.py:67
  101.3 14.5 %collective-permute-start.16 = (bf16[2,2,2,2,16,1792]{5,4,3,2,1,0:T(8,128)(2,1)S(1)}, bf16[2,2,2,2,16,1792]{5,4,3,2,1,0:T(8,128)(2,1)}, u32[]{:S(2)}, u32[]{:S(2)}) collective-permute-start(bf16[2,2,2,2,16,1792]{5,4,3,2,1,0:T(8,128)(2,1)S(1)} %pad_maximum_fusion.2.refs_4_), channel_id=1, source_target_pairs={{0,16},{1,17},{2,18},{3,19},{4,20},{5,21},{6,22},{7,23},{8,56},{9,... | collective-permute-start | bytes 2752520 | tf_op jit(solution)/shard_map/ppermute | solution.py:67
  103.5 12.3 %collective-permute-start.6 = (bf16[2,2,2,2,16,1536]{5,4,3,2,1,0:T(8,128)(2,1)S(1)}, bf16[2,2,2,2,16,1536]{5,4,3,2,1,0:T(8,128)(2,1)S(1)}, u32[]{:S(2)}, u32[]{:S(2)}) collective-permute-start(bf16[2,2,2,2,16,1536]{5,4,3,2,1,0:T(8,128)(2,1)S(1)} %pad_maximum_fusion.3.refs_0_), channel_id=1, source_target_pairs={{0,2},{1,3},{2,0},{3,1},{4,6},{5,7},{6,4},{7,5},{8,14},{9,15},{10,... | collective-permute-start | bytes 2359304 | tf_op jit(solution)/shard_map/ppermute | solution.py:67
  103.7 18.2 %collective-permute-start.5 = (bf16[2,2,2,2,16,1536]{5,4,3,2,1,0:T(8,128)(2,1)S(1)}, bf16[2,2,2,2,16,1536]{5,4,3,2,1,0:T(8,128)(2,1)}, u32[]{:S(2)}, u32[]{:S(2)}) collective-permute-start(bf16[2,2,2,2,16,1536]{5,4,3,2,1,0:T(8,128)(2,1)S(1)} %pad_maximum_fusion.3.refs_0_), channel_id=1, source_target_pairs={{0,64},{1,65},{2,66},{3,67},{4,68},{5,69},{6,70},{7,71},{8,73},{9,... | collective-permute-start | bytes 2359304 | tf_op jit(solution)/shard_map/ppermute | solution.py:67
  105.4 32.1 %collective-permute-start.18 = (bf16[2,2,2,2,16,1792]{5,4,3,2,1,0:T(8,128)(2,1)S(1)}, bf16[2,2,2,2,16,1792]{5,4,3,2,1,0:T(8,128)(2,1)}, u32[]{:S(2)}, u32[]{:S(2)}) collective-permute-start(bf16[2,2,2,2,16,1792]{5,4,3,2,1,0:T(8,128)(2,1)S(1)} %pad_maximum_fusion.1.refs_2_), channel_id=1, source_target_pairs={{0,16},{1,17},{2,18},{3,19},{4,20},{5,21},{6,22},{7,23},{8,56},{9,... | collective-permute-start | bytes 2752520 | tf_op jit(solution)/shard_map/ppermute | solution.py:67
  115.8 1.0 copy-start.2
  115.8 21.7 %collective-permute-start.20 = (bf16[2,2,2,2,16,1792]{5,4,3,2,1,0:T(8,128)(2,1)S(1)}, bf16[2,2,2,2,16,1792]{5,4,3,2,1,0:T(8,128)(2,1)}, u32[]{:S(2)}, u32[]{:S(2)}) collective-permute-start(bf16[2,2,2,2,16,1792]{5,4,3,2,1,0:T(8,128)(2,1)S(1)} %pad_maximum_fusion.2.refs_4_), channel_id=1, source_target_pairs={{0,2},{1,3},{2,0},{3,1},{4,6},{5,7},{6,4},{7,5},{8,14},{9,15},{10,... | collective-permute-start | bytes 2752520 | tf_op jit(solution)/shard_map/ppermute | solution.py:67
  116.7 20.8 %collective-permute-start.19 = (bf16[2,2,2,2,16,1792]{5,4,3,2,1,0:T(8,128)(2,1)S(1)}, bf16[2,2,2,2,16,1792]{5,4,3,2,1,0:T(8,128)(2,1)}, u32[]{:S(2)}, u32[]{:S(2)}) collective-permute-start(bf16[2,2,2,2,16,1792]{5,4,3,2,1,0:T(8,128)(2,1)S(1)} %collective-permute-done.11.refs_3_), channel_id=1, source_target_pairs={{0,16},{1,17},{2,18},{3,19},{4,20},{5,21},{6,22},{7,23},{8,56},{9,... | collective-permute-start | bytes 2752520 | tf_op jit(solution)/shard_map/ppermute | solution.py:67
  117.5 21.6 %collective-permute-start.21 = (bf16[2,2,2,2,16,1792]{5,4,3,2,1,0:T(8,128)(2,1)}, bf16[2,2,2,2,16,1792]{5,4,3,2,1,0:T(8,128)(2,1)}, u32[]{:S(2)}, u32[]{:S(2)}) collective-permute-start(bf16[2,2,2,2,16,1792]{5,4,3,2,1,0:T(8,128)(2,1)} %collective-permute-done.16.refs_5_), channel_id=1, source_target_pairs={{0,2},{1,3},{2,0},{3,1},{4,6},{5,7},{6,4},{7,5},{8,14},{9,15},{10,... | collective-permute-start | bytes 2752520 | tf_op jit(solution)/shard_map/ppermute | solution.py:67
  121.9 15.6 %collective-permute-start.17 = (bf16[2,2,2,2,16,1536]{5,4,3,2,1,0:T(8,128)(2,1)}, bf16[2,2,2,2,16,1536]{5,4,3,2,1,0:T(8,128)(2,1)}, u32[]{:S(2)}, u32[]{:S(2)}) collective-permute-start(bf16[2,2,2,2,16,1536]{5,4,3,2,1,0:T(8,128)(2,1)} %copy-done.2), channel_id=1, source_target_pairs={{0,64},{1,65},{2,66},{3,67},{4,68},{5,69},{6,70},{7,71},{8,73},{9,... | collective-permute-start | bytes 2359304 | tf_op jit(solution)/shard_map/ppermute | solution.py:67
  123.3 1.1 copy-start.3
  137.5 24.0 %copy-start.6 = (s32[32]{0:T(128)S(1)}, s32[32]{0:T(128)}, u32[]{:S(2)}) copy-start(s32[32]{0:T(128)} %get-tuple-element.22) | copy-start | bytes 388
  153.6 27.7 %collective-permute-start.22 = (f32[2,2,2,8,16,640]{5,4,3,2,1,0:T(8,128)}, f32[2,2,2,8,16,640]{5,4,3,2,1,0:T(8,128)}, u32[]{:S(2)}, u32[]{:S(2)}) collective-permute-start(f32[2,2,2,8,16,640]{5,4,3,2,1,0:T(8,128)} %get-tuple-element.24), channel_id=1, source_target_pairs={{0,8},{1,9},{2,10},{3,11},{4,12},{5,13},{6,14},{7,15},{8,0},{9,1},... | collective-permute-start | bytes 7864328 | tf_op jit(solution)/shard_map/ppermute | solution.py:58
  157.6 10.5 %all-to-all-start.2 = ((f32[8,1,1024]{2,1,0:T(1,128)}), f32[8,1,1024]{2,1,0:T(1,128)S(1)}, u32[]{:S(2)}, u32[]{:S(2)}) async-start(f32[8,1,1024]{2,1,0:T(1,128)} %broadcast_in_dim.16), calls=%async_computation.2 | async-start | bytes 65536 | tf_op jit(solution)/shard_map/all_to_all | solution.py:371
  168.9 11.2 %all-to-all-start.3 = ((f32[16,1,1056]{2,1,0:T(1,128)}), f32[16,1,1056]{2,1,0:T(1,128)S(1)}, u32[]{:S(2)}, u32[]{:S(2)}) async-start(f32[16,1,1056]{2,1,0:T(1,128)} %broadcast_in_dim.17), calls=%async_computation.3 | async-start | bytes 147456 | tf_op jit(solution)/shard_map/all_to_all | solution.py:371
  (1 other events, 0.7 us)

commit v2 on v1

--- a/solution.py
+++ b/solution.py
@@ -122,10 +122,27 @@
         fresh = jnp.dot(rows, weights[k][...], preferred_element_type=jnp.float32)
         return fresh.reshape(2, 2, 8, mine, cols)
 
+    def half_rows(k, at):
+        rows = lhs[k][at].reshape(16 * mine, -1)
+        fresh = jnp.dot(rows, weights[k][...], preferred_element_type=jnp.float32)
+        return fresh.reshape(2, 8, mine, cols)
+
+    def arrive(k):
+        for copy in copies(k):
+            copy.wait()
+
     begin(0)
     if mark == 0:
-        total[0] = product(0)
+        begin(1)
+        begin(2)
+        arrive(0)
         total[1] = jnp.zeros(total.shape[1:], jnp.float32)
+
+        def first(y, carry):
+            total[0, y] = half_rows(0, y)
+            return carry
+
+        lax.fori_loop(0, 2, first, 0)
     else:
         load = pltpu.make_async_copy(before, total, in_sem)
         load.start()
@@ -152,12 +169,29 @@
             at = pl.ds(pl.multiple_of((z * 2 + y) * 16 * mine, 16 * mine), 16 * mine)
             sums[at] = top + jnp.log(mass)
 
-    total[:, :, mark] += product(1)
-    for z in range(2):
-        finish(z, 1 - mark)
-    total[:, mark] += product(2)
-    for z in range(2):
-        finish(z, mark)
+    if mark == 0:
+
+        def second(z, carry):
+            total[z, :, 0] += half_rows(1, z)
+            return carry
+
+        def third(z, carry):
+            total[z, 0] += half_rows(2, z)
+            finish(z, 0)
+            finish(z, 1)
+            return carry
+
+        arrive(1)
+        lax.fori_loop(0, 2, second, 0)
+        arrive(2)
+        lax.fori_loop(0, 2, third, 0)
+    else:
+        total[:, :, mark] += product(1)
+        for z in range(2):
+            finish(z, 1 - mark)
+        total[:, mark] += product(2)
+        for z in range(2):
+            finish(z, mark)
     for z in range(2):
         for y in range(2):
             for copy in out_copies(z, y):

time: 190 us -> 190 us (level)
  no operation moved by 1% of the time
where the time goes in v2:
time: 190 us; the launch traced here: 189 us
  waiting for transfers between devices  49.1 us (26%)
  starting transfers between devices  45.6 us (24%)
  Pallas kernels  44.4 us (23%)
  blocking collectives  38.8 us (20%)
  local copies, waits for them, and re-layouts  5.9 us (3%)
  matrix products  2.76 us (1%)
  other arithmetic  2.09 us (1%)
    all_to_all x1, blocking collectives, on_device(): arrived = lax.all_to_all(both, 'vocab', 0, 0, tiled=True)  38.8 us
    ppermute x21, waiting for transfers between devices, meet(): lax.ppermute(part, BOTH, pairs[order[turn % 3]])  28.8 us
    ppermute x21, starting transfers between devices, meet(): lax.ppermute(part, BOTH, pairs[order[turn % 3]])  27.1 us
    pallas_call x2, Pallas kernels, call(): pl.pallas_call(functools.partial(head_kernel, mark), out_shape=out_shape,...  26.4 us
    all_to_all x2, waiting for transfers between devices, spread(): lax.all_to_all(jnp.broadcast_to(values[None], (copies,) + values.shape),...  12.3 us
    all_to_all x2, starting transfers between devices, spread(): lax.all_to_all(jnp.broadcast_to(values[None], (copies,) + values.shape),...  9.27 us
    all_to_all x1, waiting for transfers between devices, on_device(): local = lax.all_to_all(sorted_rows, 'grp', 0, 0, tiled=True)  7.95 us
    pallas_call x1, Pallas kernels, ordered_output(): pl.pallas_call(output_kernel, out_shape=jax.ShapeDtypeStruct((512, 4, wid...  7.68 us
  transfers between devices with their start and end apart: 26, of which 12 were waited for; matrix products, arithmetic and copies ran while one was open for 3% of the time, Pallas kernels for 12%

profile of v2, /device:TPU:1, one launch (start us, length us, event | category | flops | bytes accessed | tf_op | source)
XLA Modules:
  0.0 189.0 jit_solution(1730329805220843165)
XLA Ops:
  0.0 1.4 collective-permute-start
  1.4 7.1 %front.1 = (bf16[128,1408]{1,0:T(8,128)(2,1)}, s32[32]{0:T(128)}) custom-call(s32[32]{0:T(128)} %prompts.1, s32[1]{0:T(128)} %bitcast.column, bf16[32,4,5120]{2,1,0:T(4,128)(2,1)} %embedded.1, f32[1,5120]{1,0:T(1,128)} %bitcast.84, bf16[5120,512]{1,0:T(8,128)(2,1)} %query_w.1, bf16[5120,128]{1,0:T(8,128)(2,1)} %key_w.1, bf16[5120,128]{1,0:T(8,128)(2,1)} %value_w.1), custom_call_target="tpu_custom_call" | custom-call | flops 1006632960 | bytes 10000000 | tf_op jit(solution)/shard_map/front/pallas_call | solution.py:288
  8.6 5.9 %all-to-all-start = ((bf16[16,8,1408]{2,1,0:T(8,128)(2,1)}), bf16[16,8,1408]{2,1,0:T(8,128)(2,1)S(1)}, u32[]{:S(2)}, u32[]{:S(2)}) async-start(bf16[16,8,1408]{2,1,0:T(8,128)(2,1)} %bitcast.70), calls=%async_computation | async-start | bytes 720896 | tf_op jit(solution)/shard_map/all_to_all | solution.py:448
  14.4 7.9 %all-to-all-done = bf16[16,8,1408]{2,1,0:T(8,128)(2,1)S(1)} async-done(((bf16[16,8,1408]{2,1,0:T(8,128)(2,1)}), bf16[16,8,1408]{2,1,0:T(8,128)(2,1)S(1)}, u32[]{:S(2)}, u32[]{:S(2)}) %all-to-all-start) | async-done | bytes 360480 | tf_op jit(solution)/shard_map/all_to_all | solution.py:448
  22.4 3.2 %attend.1 = bf16[128,512]{1,0:T(8,128)(2,1)S(1)} custom-call(bf16[128,1408]{1,0:T(8,128)(2,1)S(1)} %bitcast.62, bf16[2048,128]{1,0:T(8,128)(2,1)S(1)} %bitcast.64, bf16[2048,128]{1,0:T(8,128)(2,1)S(1)} %bitcast.65), custom_call_target="tpu_custom_call" | custom-call | tf_op jit(solution)/shard_map/attend/pallas_call | solution.py:347
  25.6 2.2 %fusion.2 = f32[128,2560]{1,0:T(8,128)S(1)} fusion(bf16[128,512]{1,0:T(8,128)(2,1)S(1)} %attend.1, bf16[512,5120]{1,0:T(8,128)(2,1)} %param.16), kind=kOutput, calls=%fused_computation.4 | convolution fusion | flops 335544320 | bytes 4063232 | tf_op jit(solution)/shard_map/dot_general | solution.py:456
  28.7 38.8 %all_to_all.38 = f32[8,16,5120]{2,1,0:T(8,128)S(1)} all-to-all(f32[8,16,5120]{2,1,0:T(8,128)S(1)} %bitcast.66), channel_id=1, replica_groups=mesh['grp'=16,'vocab'=8] {'vocab'}, dimensions={0} | all-to-all | bytes 5242880 | tf_op jit(solution)/shard_map/all_to_all | solution.py:463
  68.4 3.1 %collective-permute-start.1 = (bf16[16,1536]{1,0:T(8,128)(2,1)S(1)}, bf16[16,1536]{1,0:T(8,128)(2,1)S(1)}, u32[]{:S(2)}, u32[]{:S(2)}) collective-permute-start(bf16[16,1536]{1,0:T(8,128)(2,1)S(1)} %get-tuple-element.44), channel_id=1, source_target_pairs={{0,32},{1,33},{2,34},{3,35},{4,36},{5,37},{6,38},{7,39},{8,40},{9,... | collective-permute-start | bytes 147464 | tf_op jit(solution)/shard_map/ppermute | solution.py:67
  73.3 2.5 %collective-permute-start.2 = (bf16[2,16,1536]{2,1,0:T(8,128)(2,1)S(1)}, bf16[2,16,1536]{2,1,0:T(8,128)(2,1)S(1)}, u32[]{:S(2)}, u32[]{:S(2)}) collective-permute-start(bf16[2,16,1536]{2,1,0:T(8,128)(2,1)S(1)} %get-tuple-element.50), channel_id=1, source_target_pairs={{0,4},{1,5},{2,6},{3,7},{4,0},{5,1},{6,2},{7,3},{8,12},{9,13},{10,... | collective-permute-start | bytes 294920 | tf_op jit(solution)/shard_map/ppermute | solution.py:67
  76.4 1.3 collective-permute-start.8
  79.1 1.6 collective-permute-start.3
  83.0 1.5 collective-permute-start.14
  84.5 4.3 %collective-permute-done.9 = bf16[2,2,16,1792]{3,2,1,0:T(8,128)(2,1)S(1)} collective-permute-done((bf16[2,2,16,1792]{3,2,1,0:T(8,128)(2,1)S(1)}, bf16[2,2,16,1792]{3,2,1,0:T(8,128)(2,1)S(1)}, u32[]{:S(2)}, u32[]{:S(2)}) %collective-permute-start.9) | collective-permute-done | bytes 229408 | tf_op jit(solution)/shard_map/ppermute | solution.py:67
  91.2 1.4 collective-permute-start.4
  92.6 7.1 %collective-permute-done.10 = bf16[2,2,2,16,1792]{4,3,2,1,0:T(8,128)(2,1)S(1)} collective-permute-done((bf16[2,2,2,16,1792]{4,3,2,1,0:T(8,128)(2,1)S(1)}, bf16[2,2,2,16,1792]{4,3,2,1,0:T(8,128)(2,1)S(1)}, u32[]{:S(2)}, u32[]{:S(2)}) %collective-permute-start.10) | collective-permute-done | bytes 458784 | tf_op jit(solution)/shard_map/ppermute | solution.py:67
  99.9 1.4 collective-permute-start.11
  101.3 2.1 %collective-permute-start.16 = (bf16[2,2,2,2,16,1792]{5,4,3,2,1,0:T(8,128)(2,1)S(1)}, bf16[2,2,2,2,16,1792]{5,4,3,2,1,0:T(8,128)(2,1)}, u32[]{:S(2)}, u32[]{:S(2)}) collective-permute-start(bf16[2,2,2,2,16,1792]{5,4,3,2,1,0:T(8,128)(2,1)S(1)} %pad_maximum_fusion.2.refs_4_), channel_id=1, source_target_pairs={{0,16},{1,17},{2,18},{3,19},{4,20},{5,21},{6,22},{7,23},{8,56},{9,... | collective-permute-start | bytes 2752520 | tf_op jit(solution)/shard_map/ppermute | solution.py:67
  103.7 1.6 collective-permute-start.5
  105.4 1.5 collective-permute-start.18
  106.9 8.9 %collective-permute-done.6.refs_1_ = bf16[2,2,2,2,16,1536]{5,4,3,2,1,0:T(8,128)(2,1)S(1)} collective-permute-done((bf16[2,2,2,2,16,1536]{5,4,3,2,1,0:T(8,128)(2,1)S(1)}, bf16[2,2,2,2,16,1536]{5,4,3,2,1,0:T(8,128)(2,1)S(1)}, u32[]{:S(2)}, u32[]{:S(2)}) %collective-permute-start.6) | collective-permute-done | bytes 786464 | tf_op jit(solution)/shard_map/ppermute | solution.py:67
  117.5 1.7 collective-permute-start.21
  119.3 2.7 %collective-permute-done.5.refs_0_ = bf16[2,2,2,2,16,1536]{5,4,3,2,1,0:T(8,128)(2,1)} collective-permute-done((bf16[2,2,2,2,16,1536]{5,4,3,2,1,0:T(8,128)(2,1)S(1)}, bf16[2,2,2,2,16,1536]{5,4,3,2,1,0:T(8,128)(2,1)}, u32[]{:S(2)}, u32[]{:S(2)}) %collective-permute-start.5) | collective-permute-done | bytes 786464 | tf_op jit(solution)/shard_map/ppermute | solution.py:67
  121.9 1.3 collective-permute-start.17
  124.4 12.0 %head_early.1.refs_8_ = f32[2,2,2,8,16,1280]{5,4,3,2,1,0:T(8,128)} custom-call(bf16[2,2,2,2,16,1536]{5,4,3,2,1,0:T(8,128)(2,1)S(1)} %pad_maximum_fusion.3.refs_0_, bf16[2,2,2,2,16,1536]{5,4,3,2,1,0:T(8,128)(2,1)S(1)} %copy-done.3, bf16[2,2,2,2,16,1792]{5,4,3,2,1,0:T(8,128)(2,1)S(1)} %pad_maximum_fusion.1.refs_2_, ...), custom_call_target="tpu_custom_call" | custom-call | flops 6710886400 | bytes 26000000 | tf_op jit(solution)/shard_map/head_early/pallas_call | solution.py:210
  136.5 2.7 %collective-permute-done.21.refs_5_ = bf16[2,2,2,2,16,1792]{5,4,3,2,1,0:T(8,128)(2,1)} collective-permute-done((bf16[2,2,2,2,16,1792]{5,4,3,2,1,0:T(8,128)(2,1)}, bf16[2,2,2,2,16,1792]{5,4,3,2,1,0:T(8,128)(2,1)}, u32[]{:S(2)}, u32[]{:S(2)}) %collective-permute-start.21) | collective-permute-done | bytes 917536 | tf_op jit(solution)/shard_map/ppermute | solution.py:67
  139.2 14.4 %head_late.1 = (f32[2,2,2,8,16,640]{5,4,3,2,1,0:T(8,128)}, f32[2,2,2,8,16,640]{5,4,3,2,1,0:T(8,128)}, f32[1024,1]{1,0:T(8,128)S(1)}) custom-call(bf16[2,2,2,2,16,1536]{5,4,3,2,1,0:T(8,128)(2,1)} %collective-permute-done.5.refs_0_, bf16[2,2,2,2,16,1536]{5,4,3,2,1,0:T(8,128)(2,1)} %collective-permute-done.17.refs_1_, ...), custom_call_target="tpu_custom_call" | custom-call | flops 6710886400 | bytes 26000000 | tf_op jit(solution)/shard_map/head_late/pallas_call | solution.py:210
  153.6 1.9 collective-permute-start.22
  157.6 3.9 %all-to-all-start.2 = ((f32[8,1,1024]{2,1,0:T(1,128)}), f32[8,1,1024]{2,1,0:T(1,128)S(1)}, u32[]{:S(2)}, u32[]{:S(2)}) async-start(f32[8,1,1024]{2,1,0:T(1,128)} %broadcast_in_dim.16), calls=%async_computation.2 | async-start | bytes 65536 | tf_op jit(solution)/shard_map/all_to_all | solution.py:405
  161.5 6.6 %all-to-all-done.2 = f32[8,1,1024]{2,1,0:T(1,128)S(1)} async-done(((f32[8,1,1024]{2,1,0:T(1,128)}), f32[8,1,1024]{2,1,0:T(1,128)S(1)}, u32[]{:S(2)}, u32[]{:S(2)}) %all-to-all-start.2) | async-done | bytes 32800 | tf_op jit(solution)/shard_map/all_to_all | solution.py:405
  168.9 5.4 %all-to-all-start.3 = ((f32[16,1,1056]{2,1,0:T(1,128)}), f32[16,1,1056]{2,1,0:T(1,128)S(1)}, u32[]{:S(2)}, u32[]{:S(2)}) async-start(f32[16,1,1056]{2,1,0:T(1,128)} %broadcast_in_dim.17), calls=%async_computation.3 | async-start | bytes 147456 | tf_op jit(solution)/shard_map/all_to_all | solution.py:405
  174.3 5.8 %all-to-all-done.3 = f32[16,1,1056]{2,1,0:T(1,128)S(1)} async-done(((f32[16,1,1056]{2,1,0:T(1,128)}), f32[16,1,1056]{2,1,0:T(1,128)S(1)}, u32[]{:S(2)}, u32[]{:S(2)}) %all-to-all-start.3) | async-done | bytes 67616 | tf_op jit(solution)/shard_map/all_to_all | solution.py:405
  181.3 7.7 %output.1 = f32[512,4,640]{2,1,0:T(4,128)} custom-call(s32[512]{0:T(512)S(1)} %reshape.282.order, s32[4]{0:T(128)S(1)} %pad_add_fusion.place, f32[2,2,2,8,16,640]{5,4,3,2,1,0:T(8,128)} %get-tuple-element.23.own, f32[2,2,2,8,16,640]{5,4,3,2,1,0:T(8,128)} %collective-permute-done.22.other, f32[16,8,16,1]{3,2,1,0:T(8,128)S(1)} %copy.24.totals), custom_call_target="tpu_custom_call" | custom-call | tf_op jit(solution)/shard_map/output/pallas_call | solution.py:379
  (97 shorter events, 17.8 us)
Async XLA Ops:
  0.0 25.6 %collective-permute-start = (bf16[5120,640]{1,0:T(8,128)(2,1)}, bf16[5120,640]{1,0:T(8,128)(2,1)}, u32[]{:S(2)}, u32[]{:S(2)}) collective-permute-start(bf16[5120,640]{1,0:T(8,128)(2,1)} %refs_6_.3), channel_id=1, source_target_pairs={{0,8},{1,9},{2,10},{3,11},{4,12},{5,13},{6,14},{7,15},{8,0},{9,1},... | collective-permute-start | bytes 19660808 | tf_op jit(solution)/shard_map/ppermute | solution.py:58
  1.4 21.0 %copy-start = (bf16[1,1,2048,128]{3,2,1,0:T(8,128)(2,1)S(1)}, bf16[1,1,2048,128]{3,2,1,0:T(8,128)(2,1)}, u32[]{:S(2)}) copy-start(bf16[1,1,2048,128]{3,2,1,0:T(8,128)(2,1)} %param.19) | copy-start | bytes 1572868
  1.4 21.0 %copy-start.1 = (bf16[1,1,2048,128]{3,2,1,0:T(8,128)(2,1)S(1)}, bf16[1,1,2048,128]{3,2,1,0:T(8,128)(2,1)}, u32[]{:S(2)}) copy-start(bf16[1,1,2048,128]{3,2,1,0:T(8,128)(2,1)} %param.20) | copy-start | bytes 1572868
  8.6 13.8 %all-to-all-start = ((bf16[16,8,1408]{2,1,0:T(8,128)(2,1)}), bf16[16,8,1408]{2,1,0:T(8,128)(2,1)S(1)}, u32[]{:S(2)}, u32[]{:S(2)}) async-start(bf16[16,8,1408]{2,1,0:T(8,128)(2,1)} %bitcast.70), calls=%async_computation | async-start | bytes 720896 | tf_op jit(solution)/shard_map/all_to_all | solution.py:448
  22.4 5.5 %copy-start.4 = (bf16[512,5120]{1,0:T(8,128)(2,1)S(1)}, bf16[512,5120]{1,0:T(8,128)(2,1)}, u32[]{:S(2)}) copy-start(bf16[512,5120]{1,0:T(8,128)(2,1)} %param.16) | copy-start | bytes 15728644
  68.4 4.9 %collective-permute-start.1 = (bf16[16,1536]{1,0:T(8,128)(2,1)S(1)}, bf16[16,1536]{1,0:T(8,128)(2,1)S(1)}, u32[]{:S(2)}, u32[]{:S(2)}) collective-permute-start(bf16[16,1536]{1,0:T(8,128)(2,1)S(1)} %get-tuple-element.44), channel_id=1, source_target_pairs={{0,32},{1,33},{2,34},{3,35},{4,36},{5,37},{6,38},{7,39},{8,40},{9,... | collective-permute-start | bytes 147464 | tf_op jit(solution)/shard_map/ppermute | solution.py:67
  71.5 4.9 %collective-permute-start.7 = (bf16[16,1792]{1,0:T(8,128)(2,1)S(1)}, bf16[16,1792]{1,0:T(8,128)(2,1)S(1)}, u32[]{:S(2)}, u32[]{:S(2)}) collective-permute-start(bf16[16,1792]{1,0:T(8,128)(2,1)S(1)} %get-tuple-element.42), channel_id=1, source_target_pairs={{0,4},{1,5},{2,6},{3,7},{4,0},{5,1},{6,2},{7,3},{8,12},{9,13},{10,... | collective-permute-start | bytes 172040 | tf_op jit(solution)/shard_map/ppermute | solution.py:67
  72.6 5.1 %collective-permute-start.12 = (bf16[16,1792]{1,0:T(8,128)(2,1)S(1)}, bf16[16,1792]{1,0:T(8,128)(2,1)S(1)}, u32[]{:S(2)}, u32[]{:S(2)}) collective-permute-start(bf16[16,1792]{1,0:T(8,128)(2,1)S(1)} %get-tuple-element.41), channel_id=1, source_target_pairs={{0,1},{1,0},{2,3},{3,2},{4,5},{5,4},{6,7},{7,6},{8,9},{9,8},{10,11... | collective-permute-start | bytes 172040 | tf_op jit(solution)/shard_map/ppermute | solution.py:67
  73.3 5.8 %collective-permute-start.2 = (bf16[2,16,1536]{2,1,0:T(8,128)(2,1)S(1)}, bf16[2,16,1536]{2,1,0:T(8,128)(2,1)S(1)}, u32[]{:S(2)}, u32[]{:S(2)}) collective-permute-start(bf16[2,16,1536]{2,1,0:T(8,128)(2,1)S(1)} %get-tuple-element.50), channel_id=1, source_target_pairs={{0,4},{1,5},{2,6},{3,7},{4,0},{5,1},{6,2},{7,3},{8,12},{9,13},{10,... | collective-permute-start | bytes 294920 | tf_op jit(solution)/shard_map/ppermute | solution.py:67
  76.4 5.5 %collective-permute-start.8 = (bf16[2,16,1792]{2,1,0:T(8,128)(2,1)S(1)}, bf16[2,16,1792]{2,1,0:T(8,128)(2,1)S(1)}, u32[]{:S(2)}, u32[]{:S(2)}) collective-permute-start(bf16[2,16,1792]{2,1,0:T(8,128)(2,1)S(1)} %get-tuple-element.48), channel_id=1, source_target_pairs={{0,1},{1,0},{2,3},{3,2},{4,5},{5,4},{6,7},{7,6},{8,9},{9,8},{10,11... | collective-permute-start | bytes 344072 | tf_op jit(solution)/shard_map/ppermute | solution.py:67
  77.8 5.2 %collective-permute-start.13 = (bf16[2,16,1792]{2,1,0:T(8,128)(2,1)S(1)}, bf16[2,16,1792]{2,1,0:T(8,128)(2,1)S(1)}, u32[]{:S(2)}, u32[]{:S(2)}) collective-permute-start(bf16[2,16,1792]{2,1,0:T(8,128)(2,1)S(1)} %get-tuple-element.46), channel_id=1, source_target_pairs={{0,32},{1,33},{2,34},{3,35},{4,36},{5,37},{6,38},{7,39},{8,40},{9,... | collective-permute-start | bytes 344072 | tf_op jit(solution)/shard_map/ppermute | solution.py:67
  79.1 12.0 %collective-permute-start.3 = (bf16[2,2,16,1536]{3,2,1,0:T(8,128)(2,1)S(1)}, bf16[2,2,16,1536]{3,2,1,0:T(8,128)(2,1)S(1)}, u32[]{:S(2)}, u32[]{:S(2)}) collective-permute-start(bf16[2,2,16,1536]{3,2,1,0:T(8,128)(2,1)S(1)} %get-tuple-element.38), channel_id=1, source_target_pairs={{0,1},{1,0},{2,3},{3,2},{4,5},{5,4},{6,7},{7,6},{8,9},{9,8},{10,11... | collective-permute-start | bytes 589832 | tf_op jit(solution)/shard_map/ppermute | solution.py:67
  82.0 6.8 %collective-permute-start.9 = (bf16[2,2,16,1792]{3,2,1,0:T(8,128)(2,1)S(1)}, bf16[2,2,16,1792]{3,2,1,0:T(8,128)(2,1)S(1)}, u32[]{:S(2)}, u32[]{:S(2)}) collective-permute-start(bf16[2,2,16,1792]{3,2,1,0:T(8,128)(2,1)S(1)} %get-tuple-element.36), channel_id=1, source_target_pairs={{0,32},{1,33},{2,34},{3,35},{4,36},{5,37},{6,38},{7,39},{8,40},{9,... | collective-permute-start | bytes 688136 | tf_op jit(solution)/shard_map/ppermute | solution.py:67
  83.0 6.8 %collective-permute-start.14 = (bf16[2,2,16,1792]{3,2,1,0:T(8,128)(2,1)S(1)}, bf16[2,2,16,1792]{3,2,1,0:T(8,128)(2,1)S(1)}, u32[]{:S(2)}, u32[]{:S(2)}) collective-permute-start(bf16[2,2,16,1792]{3,2,1,0:T(8,128)(2,1)S(1)} %get-tuple-element.34), channel_id=1, source_target_pairs={{0,4},{1,5},{2,6},{3,7},{4,0},{5,1},{6,2},{7,3},{8,12},{9,13},{10,... | collective-permute-start | bytes 688136 | tf_op jit(solution)/shard_map/ppermute | solution.py:67
  88.8 11.0 %collective-permute-start.10 = (bf16[2,2,2,16,1792]{4,3,2,1,0:T(8,128)(2,1)S(1)}, bf16[2,2,2,16,1792]{4,3,2,1,0:T(8,128)(2,1)S(1)}, u32[]{:S(2)}, u32[]{:S(2)}) collective-permute-start(bf16[2,2,2,16,1792]{4,3,2,1,0:T(8,128)(2,1)S(1)} %get-tuple-element.28), channel_id=1, source_target_pairs={{0,2},{1,3},{2,0},{3,1},{4,6},{5,7},{6,4},{7,5},{8,14},{9,15},{10,... | collective-permute-start | bytes 1376264 | tf_op jit(solution)/shard_map/ppermute | solution.py:67
  89.9 11.3 %collective-permute-start.15 = (bf16[2,2,2,16,1792]{4,3,2,1,0:T(8,128)(2,1)S(1)}, bf16[2,2,2,16,1792]{4,3,2,1,0:T(8,128)(2,1)S(1)}, u32[]{:S(2)}, u32[]{:S(2)}) collective-permute-start(bf16[2,2,2,16,1792]{4,3,2,1,0:T(8,128)(2,1)S(1)} %get-tuple-element.26), channel_id=1, source_target_pairs={{0,64},{1,65},{2,66},{3,67},{4,68},{5,69},{6,70},{7,71},{8,73},{9,... | collective-permute-start | bytes 1376264 | tf_op jit(solution)/shard_map/ppermute | solution.py:67
  91.2 12.1 %collective-permute-start.4 = (bf16[2,2,2,16,1536]{4,3,2,1,0:T(8,128)(2,1)S(1)}, bf16[2,2,2,16,1536]{4,3,2,1,0:T(8,128)(2,1)S(1)}, u32[]{:S(2)}, u32[]{:S(2)}) collective-permute-start(bf16[2,2,2,16,1536]{4,3,2,1,0:T(8,128)(2,1)S(1)} %get-tuple-element.30), channel_id=1, source_target_pairs={{0,16},{1,17},{2,18},{3,19},{4,20},{5,21},{6,22},{7,23},{8,56},{9,... | collective-permute-start | bytes 1179656 | tf_op jit(solution)/shard_map/ppermute | solution.py:67
  99.9 15.9 %collective-permute-start.11 = (bf16[2,2,2,2,16,1792]{5,4,3,2,1,0:T(8,128)(2,1)S(1)}, bf16[2,2,2,2,16,1792]{5,4,3,2,1,0:T(8,128)(2,1)S(1)}, u32[]{:S(2)}, u32[]{:S(2)}) collective-permute-start(bf16[2,2,2,2,16,1792]{5,4,3,2,1,0:T(8,128)(2,1)S(1)} %pad_maximum_fusion.1.refs_2_), channel_id=1, source_target_pairs={{0,64},{1,65},{2,66},{3,67},{4,68},{5,69},{6,70},{7,71},{8,73},{9,... | collective-permute-start | bytes 2752520 | tf_op jit(solution)/shard_map/ppermute | solution.py:67
  101.3 14.5 %collective-permute-start.16 = (bf16[2,2,2,2,16,1792]{5,4,3,2,1,0:T(8,128)(2,1)S(1)}, bf16[2,2,2,2,16,1792]{5,4,3,2,1,0:T(8,128)(2,1)}, u32[]{:S(2)}, u32[]{:S(2)}) collective-permute-start(bf16[2,2,2,2,16,1792]{5,4,3,2,1,0:T(8,128)(2,1)S(1)} %pad_maximum_fusion.2.refs_4_), channel_id=1, source_target_pairs={{0,16},{1,17},{2,18},{3,19},{4,20},{5,21},{6,22},{7,23},{8,56},{9,... | collective-permute-start | bytes 2752520 | tf_op jit(solution)/shard_map/ppermute | solution.py:67
  103.5 12.3 %collective-permute-start.6 = (bf16[2,2,2,2,16,1536]{5,4,3,2,1,0:T(8,128)(2,1)S(1)}, bf16[2,2,2,2,16,1536]{5,4,3,2,1,0:T(8,128)(2,1)S(1)}, u32[]{:S(2)}, u32[]{:S(2)}) collective-permute-start(bf16[2,2,2,2,16,1536]{5,4,3,2,1,0:T(8,128)(2,1)S(1)} %pad_maximum_fusion.3.refs_0_), channel_id=1, source_target_pairs={{0,2},{1,3},{2,0},{3,1},{4,6},{5,7},{6,4},{7,5},{8,14},{9,15},{10,... | collective-permute-start | bytes 2359304 | tf_op jit(solution)/shard_map/ppermute | solution.py:67
  103.7 18.2 %collective-permute-start.5 = (bf16[2,2,2,2,16,1536]{5,4,3,2,1,0:T(8,128)(2,1)S(1)}, bf16[2,2,2,2,16,1536]{5,4,3,2,1,0:T(8,128)(2,1)}, u32[]{:S(2)}, u32[]{:S(2)}) collective-permute-start(bf16[2,2,2,2,16,1536]{5,4,3,2,1,0:T(8,128)(2,1)S(1)} %pad_maximum_fusion.3.refs_0_), channel_id=1, source_target_pairs={{0,64},{1,65},{2,66},{3,67},{4,68},{5,69},{6,70},{7,71},{8,73},{9,... | collective-permute-start | bytes 2359304 | tf_op jit(solution)/shard_map/ppermute | solution.py:67
  105.4 31.0 %collective-permute-start.18 = (bf16[2,2,2,2,16,1792]{5,4,3,2,1,0:T(8,128)(2,1)S(1)}, bf16[2,2,2,2,16,1792]{5,4,3,2,1,0:T(8,128)(2,1)}, u32[]{:S(2)}, u32[]{:S(2)}) collective-permute-start(bf16[2,2,2,2,16,1792]{5,4,3,2,1,0:T(8,128)(2,1)S(1)} %pad_maximum_fusion.1.refs_2_), channel_id=1, source_target_pairs={{0,16},{1,17},{2,18},{3,19},{4,20},{5,21},{6,22},{7,23},{8,56},{9,... | collective-permute-start | bytes 2752520 | tf_op jit(solution)/shard_map/ppermute | solution.py:67
  115.8 1.0 copy-start.2
  115.8 20.6 %collective-permute-start.20 = (bf16[2,2,2,2,16,1792]{5,4,3,2,1,0:T(8,128)(2,1)S(1)}, bf16[2,2,2,2,16,1792]{5,4,3,2,1,0:T(8,128)(2,1)}, u32[]{:S(2)}, u32[]{:S(2)}) collective-permute-start(bf16[2,2,2,2,16,1792]{5,4,3,2,1,0:T(8,128)(2,1)S(1)} %pad_maximum_fusion.2.refs_4_), channel_id=1, source_target_pairs={{0,2},{1,3},{2,0},{3,1},{4,6},{5,7},{6,4},{7,5},{8,14},{9,15},{10,... | collective-permute-start | bytes 2752520 | tf_op jit(solution)/shard_map/ppermute | solution.py:67
  116.7 19.7 %collective-permute-start.19 = (bf16[2,2,2,2,16,1792]{5,4,3,2,1,0:T(8,128)(2,1)S(1)}, bf16[2,2,2,2,16,1792]{5,4,3,2,1,0:T(8,128)(2,1)}, u32[]{:S(2)}, u32[]{:S(2)}) collective-permute-start(bf16[2,2,2,2,16,1792]{5,4,3,2,1,0:T(8,128)(2,1)S(1)} %collective-permute-done.11.refs_3_), channel_id=1, source_target_pairs={{0,16},{1,17},{2,18},{3,19},{4,20},{5,21},{6,22},{7,23},{8,56},{9,... | collective-permute-start | bytes 2752520 | tf_op jit(solution)/shard_map/ppermute | solution.py:67
  117.5 21.6 %collective-permute-start.21 = (bf16[2,2,2,2,16,1792]{5,4,3,2,1,0:T(8,128)(2,1)}, bf16[2,2,2,2,16,1792]{5,4,3,2,1,0:T(8,128)(2,1)}, u32[]{:S(2)}, u32[]{:S(2)}) collective-permute-start(bf16[2,2,2,2,16,1792]{5,4,3,2,1,0:T(8,128)(2,1)} %collective-permute-done.16.refs_5_), channel_id=1, source_target_pairs={{0,2},{1,3},{2,0},{3,1},{4,6},{5,7},{6,4},{7,5},{8,14},{9,15},{10,... | collective-permute-start | bytes 2752520 | tf_op jit(solution)/shard_map/ppermute | solution.py:67
  121.9 14.5 %collective-permute-start.17 = (bf16[2,2,2,2,16,1536]{5,4,3,2,1,0:T(8,128)(2,1)}, bf16[2,2,2,2,16,1536]{5,4,3,2,1,0:T(8,128)(2,1)}, u32[]{:S(2)}, u32[]{:S(2)}) collective-permute-start(bf16[2,2,2,2,16,1536]{5,4,3,2,1,0:T(8,128)(2,1)} %copy-done.2), channel_id=1, source_target_pairs={{0,64},{1,65},{2,66},{3,67},{4,68},{5,69},{6,70},{7,71},{8,73},{9,... | collective-permute-start | bytes 2359304 | tf_op jit(solution)/shard_map/ppermute | solution.py:67
  123.3 1.1 copy-start.3
  136.4 25.1 %copy-start.6 = (s32[32]{0:T(128)S(1)}, s32[32]{0:T(128)}, u32[]{:S(2)}) copy-start(s32[32]{0:T(128)} %get-tuple-element.22) | copy-start | bytes 388
  153.6 27.7 %collective-permute-start.22 = (f32[2,2,2,8,16,640]{5,4,3,2,1,0:T(8,128)}, f32[2,2,2,8,16,640]{5,4,3,2,1,0:T(8,128)}, u32[]{:S(2)}, u32[]{:S(2)}) collective-permute-start(f32[2,2,2,8,16,640]{5,4,3,2,1,0:T(8,128)} %get-tuple-element.24), channel_id=1, source_target_pairs={{0,8},{1,9},{2,10},{3,11},{4,12},{5,13},{6,14},{7,15},{8,0},{9,1},... | collective-permute-start | bytes 7864328 | tf_op jit(solution)/shard_map/ppermute | solution.py:58
  157.6 10.5 %all-to-all-start.2 = ((f32[8,1,1024]{2,1,0:T(1,128)}), f32[8,1,1024]{2,1,0:T(1,128)S(1)}, u32[]{:S(2)}, u32[]{:S(2)}) async-start(f32[8,1,1024]{2,1,0:T(1,128)} %broadcast_in_dim.16), calls=%async_computation.2 | async-start | bytes 65536 | tf_op jit(solution)/shard_map/all_to_all | solution.py:405
  168.9 11.2 %all-to-all-start.3 = ((f32[16,1,1056]{2,1,0:T(1,128)}), f32[16,1,1056]{2,1,0:T(1,128)S(1)}, u32[]{:S(2)}, u32[]{:S(2)}) async-start(f32[16,1,1056]{2,1,0:T(1,128)} %broadcast_in_dim.17), calls=%async_computation.3 | async-start | bytes 147456 | tf_op jit(solution)/shard_map/all_to_all | solution.py:405
  (1 other events, 0.7 us)
